TPU v7x, 512 devices: a whole 4x8x8 slice. The times are simulated.
512 devices in a mesh: span: 8 (over y_lo, core), seq: 32 (over x, z), rep: 2 (over y_hi).
Axes of the slice: x: 4, y: 8 (y_hi: 2, y_lo: 4; y = y_hi * 4 + y_lo), z: 8, core: 2. Of those that a mesh axis runs over, the one named last changes fastest.
Arguments:
- queries: bfloat16 [16, 512, 4096], P(('rep', 'span'), 'seq'), parts along dimension 0, may hold values from -5 to 5
- keys: bfloat16 [16, 512, 4096], P(('rep', 'span'), 'seq'), parts along dimension 0, may hold values from -5 to 5
- values: bfloat16 [16, 512, 4096], P(('rep', 'span'), 'seq'), parts along dimension 0, may hold values from -6 to 6
- timesteps: int32 [16], P(('rep', 'span')), parts along dimension 0, may hold values from 0 to 999
- history: int32 [16, 256], P(('rep', 'span')), parts along dimension 0, may hold values from 0 to 1, as said below
- gate_weight: bfloat16 [256, 4096], P(None, 'seq'), may hold values from -0.375 to 0.375
Outputs:
- gated: bfloat16 [16, 512, 4096], P(('rep', 'span'), 'seq'), parts along dimension 0
There are 2 independent parts, one for each index of `rep`. A program takes and returns all parts, laid end to end along the dimension named above; an argument that names none is the same for every part. Nothing has to cross between parts.
Inputs may be any that keep to these rules, and one draw needn't show every extreme that they name: history[c, j * 32 + b] is 0 wherever j >= c; for c >= 1, history[c, (c - 1) * 32] is 1.
All inputs are finite; a program needn't handle non-finite values.
Results may differ from a plain program's by a relative error of at most 0.005.
Values may be sent and summed in bfloat16 or wider, within the bound.
A program may use at most 64 MiB of HBM per device.

v0:
```python
import math

import jax
import jax.numpy as jnp
from jax import lax
from jax.sharding import PartitionSpec as P

HD = 128
FREQ = 256


def embed(steps):
    half = FREQ // 2
    freqs = jnp.exp(-math.log(10000.0) * jnp.arange(half, dtype=jnp.float32) / half)
    angle = steps.astype(jnp.float32)[:, None] * freqs[None, :]
    return jnp.concatenate([jnp.cos(angle), jnp.sin(angle)], axis=-1)


def absorb(carry, query3, key_rows, value_rows, keymask):
    running, total, accum = carry
    heads_here = query3.shape[1]
    key3 = key_rows.reshape(key_rows.shape[0], heads_here, HD)
    value3 = value_rows.reshape(value_rows.shape[0], heads_here, HD)
    scores = jnp.einsum("qhd,khd->hqk", query3, key3, preferred_element_type=jnp.float32) * (
        1.0 / math.sqrt(HD)
    )
    scores = jnp.where(keymask[None, None, :], scores, jnp.float32(-1e30))
    newmax = jnp.maximum(running, jnp.max(scores, axis=-1))
    shrink = jnp.exp(running - newmax)
    weights = jnp.where(
        keymask[None, None, :], jnp.exp(scores - newmax[:, :, None]), jnp.float32(0.0)
    )
    total = total * shrink + jnp.sum(weights, axis=-1)
    summed = jnp.einsum(
        "hqk,khd->qhd", weights.astype(jnp.bfloat16), value3, preferred_element_type=jnp.float32
    )
    accum = accum * shrink.T[:, :, None] + summed
    return (newmax, total, accum)


def absorb_span(carry, block_row, query3, key_rows, value_rows):
    tok_dev = key_rows.shape[0] // block_row.shape[0]
    keymask = jnp.repeat(block_row, tok_dev)
    seen = jnp.any(block_row)
    return lax.cond(
        seen,
        lambda state: absorb(state, query3, key_rows, value_rows, keymask),
        lambda state: state,
        carry,
    )


def body(queries, keys, values, timesteps, history, gate_weight):
    n_span = lax.axis_size("span")
    n_seq = lax.axis_size("seq")
    span = lax.axis_index("span")
    blocks = history[0].reshape(n_span, n_seq)
    own = (jnp.arange(n_span, dtype=jnp.int32) == span).astype(jnp.int32)[:, None]
    visible_blocks = blocks + own > 0
    gate = jnp.dot(
        embed(timesteps).astype(jnp.bfloat16), gate_weight, preferred_element_type=jnp.float32
    )[0]
    heads_here = gate_weight.shape[1] // HD
    key_all, value_all = (
        lax.all_gather(keys, "span", axis=0, tiled=True),
        lax.all_gather(values, "span", axis=0, tiled=True),
    )
    query_h, key_h, value_h = (
        lax.all_to_all(queries, "seq", split_axis=2, concat_axis=1, tiled=True),
        lax.all_to_all(key_all, "seq", split_axis=2, concat_axis=1, tiled=True),
        lax.all_to_all(value_all, "seq", split_axis=2, concat_axis=1, tiled=True),
    )
    tok_span = query_h.shape[1]
    query3 = query_h[0].reshape(tok_span, heads_here, HD)
    carry = (
        jnp.full((heads_here, tok_span), -1e30, jnp.float32),
        jnp.zeros((heads_here, tok_span), jnp.float32),
        jnp.zeros((tok_span, heads_here, HD), jnp.float32),
    )
    for source in range(n_span):
        carry = absorb_span(carry, visible_blocks[source], query3, key_h[source], value_h[source])
    running, total, accum = carry
    attended = accum / total.T[:, :, None]
    attended = attended.reshape(tok_span, heads_here * HD)
    gated = (attended * gate[None, :]).astype(jnp.bfloat16)[None]
    return lax.all_to_all(gated, "seq", split_axis=1, concat_axis=2, tiled=True)


def solution(mesh):
    return jax.shard_map(
        body,
        mesh=mesh,
        in_specs=(
            P(("rep", "span"), "seq", None),
            P(("rep", "span"), "seq", None),
            P(("rep", "span"), "seq", None),
            P(("rep", "span")),
            P(("rep", "span"), None),
            P(None, "seq"),
        ),
        out_specs=P(("rep", "span"), "seq", None),
        check_vma=False,
    )
```

profile of v0, /device:TPU:57, one launch (start us, length us, event | category | flops | bytes accessed | tf_op | source)
XLA Modules:
  0.0 262.4 jit_solution(15140211011149143651)
XLA Ops:
  6.5 0.7 all-gather.3.cloned.1.call-update
  7.3 4.3 %copy.79 = bf16[1,16,4096]{1,0,2:T(2,128)(2,1)S(1)} copy(bf16[1,16,4096]{2,1,0:T(8,128)(2,1)} %param.22) | data formatting | bytes 262144 | tf_op args[0]
  12.1 22.4 %reduce.44 = bf16[4096,16]{1,0:T(8,128)(2,1)S(1)} reduce(bf16[4096,1,16]{2,1,0:T(2,128)(2,1)S(1)} %bitcast.272, bf16[]{:T(256)} %broadcast.209), dimensions={1}, to_apply=%bitcast.209.reduce_sub_computation | reduce | bytes 262146
  34.5 1.8 reshape.404
  36.3 12.9 %all-to-all-start = ((bf16[32,2,1024]{2,1,0:T(2,128)(2,1)}), bf16[32,2,1024]{2,1,0:T(2,128)(2,1)S(1)}, u32[]{:S(2)}, u32[]{:S(2)}) async-start(bf16[32,2,1024]{2,1,0:T(2,128)(2,1)} %reshape.404), calls=%async_computation | async-start | bytes 262144 | tf_op jit(solution)/shard_map/all_to_all | solution.py:69
  49.2 4.7 %all-gather.3.cloned.1.call-done = bf16[8,16,4096]{2,1,0:T(8,128)(2,1)} async-done(((bf16[1,16,4096]{2,1,0:T(8,128)(2,1)}), bf16[8,16,4096]{2,1,0:T(8,128)(2,1)}) %all-gather.3.cloned.1.call-update) | async-done | bytes 1048592 | tf_op jit(solution)/shard_map/all_gather | solution.py:65
  53.9 8.2 %copy.82 = bf16[8,16,4096]{1,0,2:T(8,128)(2,1)} copy(bf16[8,16,4096]{2,1,0:T(8,128)(2,1)} %all-gather.3.cloned.1.call-done) | data formatting | bytes 2097152 | tf_op jit(solution)/shard_map/all_gather | solution.py:65
  62.1 11.2 %reshape.406 = bf16[32,2,8192]{2,1,0:T(2,128)(2,1)} reshape(bf16[4096,8,16]{2,1,0:T(8,128)(2,1)} %bitcast.254) | data formatting | bytes 2097152
  73.3 9.9 %all-to-all-start.1 = ((bf16[32,2,8192]{2,1,0:T(2,128)(2,1)}), bf16[32,2,8192]{2,1,0:T(2,128)(2,1)S(1)}, u32[]{:S(2)}, u32[]{:S(2)}) async-start(bf16[32,2,8192]{2,1,0:T(2,128)(2,1)} %reshape.406), calls=%async_computation.1 | async-start | bytes 2097152 | tf_op jit(solution)/shard_map/all_to_all | solution.py:70
  83.3 0.7 all-gather.5.cloned.1.call-update
  84.0 41.0 %all-gather.5.cloned.1.call-done = bf16[8,16,4096]{2,1,0:T(8,128)(2,1)} async-done(((bf16[1,16,4096]{2,1,0:T(8,128)(2,1)}), bf16[8,16,4096]{2,1,0:T(8,128)(2,1)}) %all-gather.5.cloned.1.call-update) | async-done | bytes 1048592 | tf_op jit(solution)/shard_map/all_gather | solution.py:66
  125.0 8.2 %copy.85 = bf16[8,16,4096]{1,0,2:T(8,128)(2,1)} copy(bf16[8,16,4096]{2,1,0:T(8,128)(2,1)} %all-gather.5.cloned.1.call-done) | data formatting | bytes 2097152 | tf_op jit(solution)/shard_map/all_gather | solution.py:66
  133.2 11.2 %reshape.408 = bf16[32,2,8192]{2,1,0:T(2,128)(2,1)} reshape(bf16[4096,8,16]{2,1,0:T(8,128)(2,1)} %bitcast.255) | data formatting | bytes 2097152
  144.4 10.0 %all-to-all-start.2 = ((bf16[32,2,8192]{2,1,0:T(2,128)(2,1)}), bf16[32,2,8192]{2,1,0:T(2,128)(2,1)}, u32[]{:S(2)}, u32[]{:S(2)}) async-start(bf16[32,2,8192]{2,1,0:T(2,128)(2,1)} %reshape.408), calls=%async_computation.2 | async-start | bytes 2097152 | tf_op jit(solution)/shard_map/all_to_all | solution.py:71
  155.7 0.8 fusion.103
  162.4 1.8 reshape.405
  164.3 2.0 copy.80
  166.4 8.9 %reshape.407 = bf16[4096,8,16]{2,1,0:T(8,128)(2,1)} reshape(bf16[32,2,8192]{2,1,0:T(2,128)(2,1)} %copy-done.1) | data formatting | bytes 2097152
  175.3 7.6 %copy.103 = bf16[8,16,32,128]{3,2,1,0:T(8,128)(2,1)S(1)} copy(bf16[8,16,32,128]{1,0,3,2:T(8,128)(2,1)} %bitcast.256) | data formatting | bytes 2097152 | tf_op jit(solution)/shard_map/all_to_all | solution.py:70
  183.0 0.7 copy.84
  183.7 8.9 %reshape.409 = bf16[4096,8,16]{2,1,0:T(8,128)(2,1)} reshape(bf16[32,2,8192]{2,1,0:T(2,128)(2,1)} %all-to-all-done.2) | data formatting | bytes 2097152
  192.6 7.6 %copy.104 = bf16[8,16,32,128]{3,2,1,0:T(8,128)(2,1)S(1)} copy(bf16[8,16,32,128]{1,0,3,2:T(8,128)(2,1)} %bitcast.257) | data formatting | bytes 2097152 | tf_op jit(solution)/shard_map/all_to_all | solution.py:71
  200.3 0.7 copy.87
  201.0 0.7 copy.88
  201.7 0.7 copy.89
  203.6 4.9 %conditional.8 = (f32[1,512]{1,0:T(1,128)}, f32[1,512]{1,0:T(1,128)S(1)}, f32[512,1,128]{2,0,1:T(8,128)S(1)}) conditional(s32[]{:T(128)} %convert_element_type.88, () %tuple.56, (pred[32,16]{1,0:T(8,128)(4,1)S(1)}, bf16[512,1,128]{2,0,1:T(8,128)(2,1)S(1)}, bf16[1,512,128]{2,1,0:T(8,128)(2,1)}, bf16[1,512,128]{2,1,0:T(8,128)(2,1)}) %tuple.182), branch_computations={%region_8.0_spmd, %region_9.12_spmd} | conditional | flops 136644608 | bytes 3826200 | solution.py:45
  203.7 1.2 fusion.93
  205.5 0.9 fusion.4
  207.1 1.4 fusion.2
  208.5 5.0 %conditional.9 = ((f32[1,512]{1,0:T(1,128)}, f32[1,512]{1,0:T(1,128)S(1)}, f32[512,1,128]{2,0,1:T(8,128)S(1)})) conditional(s32[]{:T(128)} %convert_element_type.87, (f32[1,512]{1,0:T(1,128)}, f32[1,512]{1,0:T(1,128)S(1)}, f32[512,1,128]{2,0,1:T(8,128)S(1)}) %conditional.8, (pred[32,16]{1,0:T(8,128)(4,1)S(1)}, bf16[512,1,128]{2,0,1:T(8,128)(2,1)S(1)}, ...), branch_computations={%region_12.13_spmd, %region_13.16_spmd} | conditional | flops 136709120 | bytes 4098592 | solution.py:45
  208.6 1.2 fusion.94
  210.8 0.7 multiply_add_fusion.1
  211.4 1.5 fusion.14
  213.6 4.1 %conditional.10 = ((f32[1,512]{1,0:T(1,128)}, f32[1,512]{1,0:T(1,128)S(1)}, f32[512,1,128]{2,0,1:T(8,128)S(1)})) conditional(s32[]{:T(128)} %convert_element_type.86, (f32[1,512]{1,0:T(1,128)}, f32[1,512]{1,0:T(1,128)S(1)}, f32[512,1,128]{2,0,1:T(8,128)S(1)}) %get-tuple-element.448, (pred[32,16]{1,0:T(8,128)(4,1)S(1)}, ...), branch_computations={%region_16.17_spmd, %region_17.20_spmd} | conditional | flops 136709120 | bytes 4098592 | solution.py:45
  214.9 0.7 multiply_add_fusion.2
  215.6 1.4 fusion.26
  217.7 3.2 %conditional.11 = ((f32[1,512]{1,0:T(1,128)}, f32[1,512]{1,0:T(1,128)S(1)}, f32[512,1,128]{2,0,1:T(8,128)S(1)})) conditional(s32[]{:T(128)} %convert_element_type.85, (f32[1,512]{1,0:T(1,128)}, f32[1,512]{1,0:T(1,128)S(1)}, f32[512,1,128]{2,0,1:T(8,128)S(1)}) %get-tuple-element.449, (pred[32,16]{1,0:T(8,128)(4,1)S(1)}, ...), branch_computations={%region_20.21_spmd, %region_21.24_spmd} | conditional | flops 136709120 | bytes 4098592 | solution.py:45
  219.0 0.7 multiply_add_fusion.3
  220.9 3.2 %conditional.12 = ((f32[1,512]{1,0:T(1,128)}, f32[1,512]{1,0:T(1,128)S(1)}, f32[512,1,128]{2,0,1:T(8,128)S(1)})) conditional(s32[]{:T(128)} %convert_element_type.84, (f32[1,512]{1,0:T(1,128)}, f32[1,512]{1,0:T(1,128)S(1)}, f32[512,1,128]{2,0,1:T(8,128)S(1)}) %get-tuple-element.450, (pred[32,16]{1,0:T(8,128)(4,1)S(1)}, ...), branch_computations={%region_24.0_spmd, %region_25.28_spmd} | conditional | flops 136709120 | bytes 4098592 | solution.py:45
  222.3 0.7 multiply_add_fusion.4
  224.2 3.3 %conditional.13 = ((f32[1,512]{1,0:T(1,128)}, f32[1,512]{1,0:T(1,128)S(1)}, f32[512,1,128]{2,0,1:T(8,128)S(1)})) conditional(s32[]{:T(128)} %convert_element_type.83, (f32[1,512]{1,0:T(1,128)}, f32[1,512]{1,0:T(1,128)S(1)}, f32[512,1,128]{2,0,1:T(8,128)S(1)}) %get-tuple-element.451, (pred[32,16]{1,0:T(8,128)(4,1)S(1)}, ...), branch_computations={%region_28.0_spmd, %region_29.32_spmd} | conditional | flops 136709120 | bytes 4098592 | solution.py:45
  225.7 0.7 multiply_add_fusion.5
  227.5 4.1 %conditional.14 = ((f32[1,512]{1,0:T(1,128)}, f32[1,512]{1,0:T(1,128)S(1)}, f32[512,1,128]{2,0,1:T(8,128)S(1)})) conditional(s32[]{:T(128)} %convert_element_type.82, (f32[1,512]{1,0:T(1,128)}, f32[1,512]{1,0:T(1,128)S(1)}, f32[512,1,128]{2,0,1:T(8,128)S(1)}) %get-tuple-element.452, (pred[1,32]{1,0:T(4,128)(4,1)S(1)}, ...), branch_computations={%region_32.33_spmd, %region_33.36_spmd} | conditional | flops 136709120 | bytes 8817728 | solution.py:45
  229.3 0.7 multiply_add_fusion.6
  231.6 3.5 %conditional.15 = ((f32[1,512]{1,0:T(1,128)S(1)}, f32[512,1,128]{2,0,1:T(8,128)S(1)})) conditional(s32[]{:T(128)} %convert_element_type.81, (f32[1,512]{1,0:T(1,128)S(1)}, f32[512,1,128]{2,0,1:T(8,128)S(1)}) %tuple.64, (pred[1,32]{1,0:T(4,128)(4,1)S(1)}, bf16[512,1,128]{2,0,1:T(8,128)(2,1)S(1)}, bf16[8,32,16,128]{3,1,2,0:T(8,128)(2,1)S(1)}, ...), branch_computations={%region_36.37_spmd, %region_37.40_spmd} | conditional | flops 136709120 | bytes 8813624 | solution.py:45
  233.4 0.7 multiply_add_fusion.7
  235.5 1.4 reduce.45
  236.9 17.9 %all_to_all.63 = bf16[32,2,1024]{2,1,0:T(2,128)(2,1)S(1)} all-to-all(bf16[32,2,1024]{2,1,0:T(2,128)(2,1)S(1)} %reshape.410), channel_id=1, replica_groups=mesh['span'=8,'seq'=32,'rep'=2] {'seq'}, dimensions={0} | all-to-all | bytes 262144 | tf_op jit(solution)/shard_map/all_to_all | solution.py:86
  (97 shorter events, 23.4 us)
Async XLA Ops:
  6.5 155.8 %copy-start = (bf16[256,128]{1,0:T(8,128)(2,1)S(1)}, bf16[256,128]{1,0:T(8,128)(2,1)}, u32[]{:S(2)}) copy-start(bf16[256,128]{1,0:T(8,128)(2,1)} %param.27) | copy-start | bytes 196612
  6.5 47.4 %all-gather.3.cloned.1.call-start = ((), (), s32[]{:S(2)}) async-start(), calls=%async_computation.4 | async-start | bytes 1179648 | tf_op jit(solution)/shard_map/all_gather | solution.py:65
  36.3 37.0 %all-to-all-start = ((bf16[32,2,1024]{2,1,0:T(2,128)(2,1)}), bf16[32,2,1024]{2,1,0:T(2,128)(2,1)S(1)}, u32[]{:S(2)}, u32[]{:S(2)}) async-start(bf16[32,2,1024]{2,1,0:T(2,128)(2,1)} %reshape.404), calls=%async_computation | async-start | bytes 262144 | tf_op jit(solution)/shard_map/all_to_all | solution.py:69
  73.3 71.1 %all-to-all-start.1 = ((bf16[32,2,8192]{2,1,0:T(2,128)(2,1)}), bf16[32,2,8192]{2,1,0:T(2,128)(2,1)S(1)}, u32[]{:S(2)}, u32[]{:S(2)}) async-start(bf16[32,2,8192]{2,1,0:T(2,128)(2,1)} %reshape.406), calls=%async_computation.1 | async-start | bytes 2097152 | tf_op jit(solution)/shard_map/all_to_all | solution.py:70
  83.3 41.7 %all-gather.5.cloned.1.call-start = ((), (), s32[]{:S(2)}) async-start(), calls=%async_computation.5 | async-start | bytes 1179648 | tf_op jit(solution)/shard_map/all_gather | solution.py:66
  84.0 70.9 %copy-start.2 = (s32[1,256]{1,0:T(1,128)S(1)}, s32[1,256]{1,0:T(1,128)}, u32[]{:S(2)}) copy-start(s32[1,256]{1,0:T(1,128)} %param.26) | copy-start | bytes 3076
  144.4 17.9 %copy-start.1 = (bf16[32,2,8192]{2,1,0:T(2,128)(2,1)}, bf16[32,2,8192]{2,1,0:T(2,128)(2,1)S(1)}, u32[]{:S(2)}) copy-start(bf16[32,2,8192]{2,1,0:T(2,128)(2,1)S(1)} %all-to-all-done.1) | copy-start | bytes 3145732
  144.4 39.3 %all-to-all-start.2 = ((bf16[32,2,8192]{2,1,0:T(2,128)(2,1)}), bf16[32,2,8192]{2,1,0:T(2,128)(2,1)}, u32[]{:S(2)}, u32[]{:S(2)}) async-start(bf16[32,2,8192]{2,1,0:T(2,128)(2,1)} %reshape.408), calls=%async_computation.2 | async-start | bytes 2097152 | tf_op jit(solution)/shard_map/all_to_all | solution.py:71
Sparse Core Ops, SparseCore 0:
  9.4 44.4 all-gather.2
  86.2 38.7 all-gather.4
where the time goes:
time: 265 us; the launch traced here: 262 us
  local copies, waits for them, and re-layouts  94.4 us (36%)
  waiting for transfers between devices  47.1 us (18%)
  other arithmetic  39 us (15%)
  starting transfers between devices  32.8 us (12%)
  between operations  19.3 us (7%)
  blocking collectives  17.9 us (7%)
  matrix products  11.5 us (4%)
    unnamed x19, local copies, waits for them, and re-layouts  49.4 us
    all_gather x1, waiting for transfers between devices, body(): lax.all_gather(values, 'span', axis=0, tiled=True)  41 us
    unnamed x4, other arithmetic  24.6 us
    all_to_all x1, blocking collectives, body(): return lax.all_to_all(gated, 'seq', split_axis=1, concat_axis=2, tiled=True)  17.9 us
    all_to_all x1, starting transfers between devices, body(): lax.all_to_all(queries, 'seq', split_axis=2, concat_axis=1, tiled=True)  12.9 us
    all_to_all x1, starting transfers between devices, body(): lax.all_to_all(value_all, 'seq', split_axis=2, concat_axis=1, tiled=True)  9.96 us
    all_to_all x1, starting transfers between devices, body(): lax.all_to_all(key_all, 'seq', split_axis=2, concat_axis=1, tiled=True)  9.92 us
    all_gather x1, local copies, waits for them, and re-layouts, body(): lax.all_gather(keys, 'span', axis=0, tiled=True)  8.22 us
  transfers between devices with their start and end apart: 5, of which 2 were waited for; matrix products, arithmetic and copies ran while one was open for 35% of the time, Pallas kernels for 0%

commit v1 on v0

v1 whole, which is shorter than its diff:
```python
import functools
import math

import jax
import jax.numpy as jnp
from jax import lax
from jax.experimental import pallas as pl
from jax.experimental.pallas import tpu as pltpu
from jax.sharding import PartitionSpec as P

HD = 128
FREQ = 256
RAISE = math.log2(math.e) / math.sqrt(HD)
HIDDEN = -1e30


def kernel(
    n_span, n_x, n_z, tok,
    q_hbm, k_hbm, v_hbm, steps_ref, history_ref, gatew_ref,
    out_ref,
    q_in, k_in, v_in, kv_stage, q_stage, kv, qbuf, obuf, bias, gate_row, top, total, accum,
    in_sem, kv_recv, kv_send, q_recv, q_send, down_send, side_send, o_recv, o_send,
):
    n_seq = n_x * n_z
    rows = n_z * tok
    n_chip = n_span // 2
    span, seq = lax.axis_index("span"), lax.axis_index("seq")
    chip, core = span // 2, lax.rem(span, 2)
    x, z = seq // n_z, lax.rem(seq, n_z)
    x_off = [0, 1, 3, 2] if n_x == 4 else list(range(n_x))

    def z_off(r):
        return jnp.where(lax.rem(r, 2) == 1, (r + 1) // 2, n_z - r // 2)

    def ahead(g, r):
        return lax.rem(x + x_off[g], n_x) * n_z + lax.rem(z + z_off(r), n_z)

    def behind(g, r):
        return lax.rem(x + n_x - x_off[g], n_x) * n_z + lax.rem(z + 2 * n_z - z_off(r), n_z)

    fetch = [
        pltpu.make_async_copy(src.at[0], dst, in_sem.at[i])
        for i, (src, dst) in enumerate(((k_hbm, k_in), (v_hbm, v_in), (q_hbm, q_in)))
    ]
    for copy in fetch:
        copy.start()
    barrier = pltpu.get_barrier_semaphore()

    @pl.loop(1, n_seq)
    def _(d):
        pl.semaphore_signal(barrier, inc=1, device_id={"seq": lax.rem(seq + d, n_seq)})

    sibling = span + 1 - 2 * core
    pl.semaphore_signal(barrier, inc=1, device_id={"span": sibling})

    @pl.when(chip > 0)
    def _():
        pl.semaphore_signal(barrier, inc=1, device_id={"span": span - 2})

    @pl.when(chip < n_chip - 1)
    def _():
        pl.semaphore_signal(barrier, inc=1, device_id={"span": span + 2})

    fetch[0].wait()
    for t in range(n_seq):
        kv_stage[t, 0] = k_in[:, t * HD : (t + 1) * HD]
    fetch[1].wait()
    for t in range(n_seq):
        kv_stage[t, 1] = v_in[:, t * HD : (t + 1) * HD]
    fetch[2].wait()
    for t in range(n_seq):
        q_stage[t] = q_in[:, t * HD : (t + 1) * HD]

    kv[span, 0, :, 0:tok, :] = kv_stage[seq]
    qbuf[0, 0:tok, :] = q_stage[seq]

    others = n_seq + (chip > 0).astype(jnp.int32) + (chip < n_chip - 1).astype(jnp.int32)
    pl.semaphore_wait(barrier, others)

    for g in range(n_x):

        @pl.loop(1 if g == 0 else 0, n_z)
        def _(r):
            to = ahead(g, r)
            pltpu.make_async_remote_copy(
                src_ref=kv_stage.at[to],
                dst_ref=kv.at[span, g, :, pl.ds(pl.multiple_of(r * tok, tok), tok), :],
                send_sem=kv_send,
                recv_sem=kv_recv.at[span, g],
                device_id={"seq": to},
            ).start()

    for g in range(n_x):

        @pl.loop(1 if g == 0 else 0, n_z)
        def _(r):
            to = ahead(g, r)
            pltpu.make_async_remote_copy(
                src_ref=q_stage.at[to],
                dst_ref=qbuf.at[g, pl.ds(pl.multiple_of(r * tok, tok), tok), :],
                send_sem=q_send,
                recv_sem=q_recv,
                device_id={"seq": to},
            ).start()

    half = FREQ // 2
    k_index = lax.broadcasted_iota(jnp.int32, (8, half), 1).astype(jnp.float32)
    freqs = jnp.exp(-math.log(10000.0) * k_index / half)
    angle = steps_ref[0].astype(jnp.float32) * freqs
    embedding = jnp.concatenate([jnp.cos(angle), jnp.sin(angle)], axis=-1).astype(jnp.bfloat16)
    gate_row[...] = jnp.dot(embedding, gatew_ref[...], preferred_element_type=jnp.float32)

    n_block = n_span * n_seq
    spread = jnp.where(
        lax.broadcasted_iota(jnp.int32, (n_span, n_block), 1) // n_seq
        == lax.broadcasted_iota(jnp.int32, (n_span, n_block), 0),
        history_ref[...],
        0,
    ).astype(jnp.float32).astype(jnp.bfloat16)
    key_at = lax.broadcasted_iota(jnp.int32, (1, n_seq * tok), 1)
    key_g, key_r = key_at // rows, lax.rem(key_at, rows) // tok
    key_dx = jnp.where(key_g == 2, 3, jnp.where(key_g == 3, 2, key_g)) if n_x == 4 else key_g
    key_block = lax.rem(x + n_x - key_dx, n_x) * n_z + lax.rem(z + 2 * n_z - z_off(key_r), n_z)
    place = lax.rem(lax.broadcasted_iota(jnp.int32, (n_block, n_seq * tok), 0), n_seq) == key_block
    shown = jnp.dot(
        spread, jnp.where(place, 1.0, 0.0).astype(jnp.bfloat16), preferred_element_type=jnp.float32
    )
    own = lax.broadcasted_iota(jnp.int32, shown.shape, 0) == span
    bias[...] = jnp.where(own | (shown > 0.5), 0.0, HIDDEN)

    def chunk_copy(j, g, sems, to):
        return pltpu.make_async_remote_copy(
            src_ref=kv.at[j, g],
            dst_ref=kv.at[j, g],
            send_sem=sems.at[j, g],
            recv_sem=kv_recv.at[j, g],
            device_id={"span": to},
        )

    def pass_on(j, g):
        @pl.when(chip < n_chip - 1)
        def _():
            chunk_copy(j, g, down_send, span + 2).start()

    def pass_aside(j, g):
        chunk_copy(j, g, side_send, sibling).start()

    def await_chunk(j, g, first=0):
        ref = kv.at[j, g, :, first:rows, :]
        pltpu.make_async_copy(ref, ref, kv_recv.at[j, g]).wait()

    def absorb(j, start):
        keys = kv[j, :, 0].reshape(n_seq * tok, HD)
        values = kv[j, :, 1].reshape(n_seq * tok, HD)
        shade = bias[pl.ds(j, 1), :]
        for g in range(n_x):
            at = slice(g * rows, (g + 1) * rows)
            scores = lax.dot_general(
                qbuf[g], keys, (((1,), (1,)), ((), ())), preferred_element_type=jnp.float32
            )
            if not start:
                scores = scores + shade
            largest = jnp.max(scores, axis=-1, keepdims=True)
            if not start:
                largest = jnp.maximum(largest, top[at, 0:1])
            weights = jnp.exp2((scores - largest) * RAISE)
            summed = jnp.dot(weights.astype(jnp.bfloat16), values, preferred_element_type=jnp.float32)
            added = jnp.sum(weights, axis=-1, keepdims=True)
            if not start:
                shrink = jnp.exp2((top[at, 0:1] - largest) * RAISE)
                summed = accum[at, :] * shrink + summed
                added = total[at, 0:1] * shrink + added
            top[at, 0:1] = largest
            total[at, 0:1] = added
            accum[at, :] = summed

    for g in range(n_x):
        await_chunk(span, g, tok if g == 0 else 0)
        pass_on(span, g)

        @pl.when(core == 0)
        def _():
            pass_aside(span, g)

    def take(h):
        @pl.when(chip >= h)
        def _():
            for g in range(n_x):
                await_chunk(span - 2 * h, g)
                pass_on(span - 2 * h, g)
                pass_aside(span - 2 * h, g)

    def from_side(h):
        def run():
            j = sibling - 2 * h
            for g in range(n_x):
                await_chunk(j, g)
            absorb(j, False)

        if h == 0:
            pl.when(core == 1)(run)
        else:
            pl.when(chip >= h)(run)

    take(1)
    q_rest = q_stage.at[1:n_seq]
    pltpu.make_async_copy(q_rest, q_rest, q_recv).wait()
    absorb(span, True)
    from_side(0)
    for h in range(1, n_chip):
        if h + 1 < n_chip:
            take(h + 1)

        @pl.when(chip >= h)
        def _():
            absorb(span - 2 * h, False)

        from_side(h)

    for g in range(n_x):
        at = slice(g * rows, (g + 1) * rows)
        attended = accum[at, :] / total[at, 0:1]
        obuf[at, :] = (attended * gate_row[0:1, :]).astype(jnp.bfloat16)
        if g == 0:
            out_ref[0, :, pl.ds(pl.multiple_of(seq * HD, HD), HD)] = obuf[0:tok, :]

        @pl.loop(1 if g == 0 else 0, n_z)
        def _(r):
            pltpu.make_async_remote_copy(
                src_ref=obuf.at[pl.ds(pl.multiple_of(g * rows + r * tok, tok), tok), :],
                dst_ref=out_ref.at[0, :, pl.ds(pl.multiple_of(seq * HD, HD), HD)],
                send_sem=o_send,
                recv_sem=o_recv,
                device_id={"seq": behind(g, r)},
            ).start()

    def drain(ref, sem):
        pltpu.make_async_copy(ref, ref, sem).wait()

    drain(kv_stage.at[1:n_seq], kv_send)
    drain(q_stage.at[1:n_seq], q_send)
    for h in range(n_chip):

        @pl.when((chip >= h) & (chip < n_chip - 1))
        def _():
            for g in range(n_x):
                chunk_copy(span - 2 * h, g, down_send, span + 2).wait_send()

        @pl.when((chip >= h) & ((core == 0) | (h > 0)))
        def _():
            for g in range(n_x):
                chunk_copy(span - 2 * h, g, side_send, sibling).wait_send()

    drain(obuf.at[tok:, :], o_send)
    drain(out_ref.at[0, :, 0 : (n_seq - 1) * HD], o_recv)


def body(queries, keys, values, timesteps, history, gate_weight):
    n_span, n_seq = lax.axis_size("span"), lax.axis_size("seq")
    n_x = 4 if n_seq == 32 else 2
    n_z = n_seq // n_x
    tok, width = queries.shape[1], queries.shape[2]
    bf16, f32 = jnp.bfloat16, jnp.float32
    rows = n_z * tok
    whole = n_seq * tok
    anywhere = pl.BlockSpec(memory_space=pl.ANY)
    vmem = pl.BlockSpec(memory_space=pltpu.VMEM)
    return pl.pallas_call(
        functools.partial(kernel, n_span, n_x, n_z, tok),
        out_shape=jax.ShapeDtypeStruct(queries.shape, bf16),
        in_specs=[anywhere] * 3 + [pl.BlockSpec(memory_space=pltpu.SMEM), vmem, vmem],
        out_specs=vmem,
        scratch_shapes=[
            pltpu.VMEM((tok, width), bf16),
            pltpu.VMEM((tok, width), bf16),
            pltpu.VMEM((tok, width), bf16),
            pltpu.VMEM((n_seq, 2, tok, HD), bf16),
            pltpu.VMEM((n_seq, tok, HD), bf16),
            pltpu.VMEM((n_span, n_x, 2, rows, HD), bf16),
            pltpu.VMEM((n_x, rows, HD), bf16),
            pltpu.VMEM((whole, HD), bf16),
            pltpu.VMEM((n_span, whole), f32),
            pltpu.VMEM((8, HD), f32),
            pltpu.VMEM((whole, HD), f32),
            pltpu.VMEM((whole, HD), f32),
            pltpu.VMEM((whole, HD), f32),
            pltpu.SemaphoreType.DMA((3,)),
            pltpu.SemaphoreType.DMA((n_span, n_x)),
            pltpu.SemaphoreType.DMA,
            pltpu.SemaphoreType.DMA,
            pltpu.SemaphoreType.DMA,
            pltpu.SemaphoreType.DMA((n_span, n_x)),
            pltpu.SemaphoreType.DMA((n_span, n_x)),
            pltpu.SemaphoreType.DMA,
            pltpu.SemaphoreType.DMA,
        ],
        compiler_params=pltpu.CompilerParams(collective_id=0, has_side_effects=True, vmem_limit_bytes=60 * 2**20),
        name="attention",
    )(queries, keys, values, timesteps, history, gate_weight)


def solution(mesh):
    return jax.shard_map(
        body,
        mesh=mesh,
        in_specs=(
            P(("rep", "span"), "seq", None),
            P(("rep", "span"), "seq", None),
            P(("rep", "span"), "seq", None),
            P(("rep", "span")),
            P(("rep", "span"), None),
            P(None, "seq"),
        ),
        out_specs=P(("rep", "span"), "seq", None),
        check_vma=False,
    )
```

time: 265 us -> 54.8 us (0.21)
  the two profiles are of different devices: /device:TPU:57 before, /device:TPU:56 now
where the time goes in v1:
time: 54.8 us; the launch traced here: 54.6 us
  Pallas kernels  52.4 us (96%)
  local copies, waits for them, and re-layouts  1.57 us (3%)
  between operations  0.66 us (1%)
    pallas_call x1, Pallas kernels, body(): pl.pallas_call(functools.partial(kernel, n_span, n_x, n_z, tok), out_shap...  52.4 us
    unnamed x1, local copies, waits for them, and re-layouts  1.57 us

profile of v1, /device:TPU:56, one launch (start us, length us, event | category | flops | bytes accessed | tf_op | source)
XLA Modules:
  0.0 54.6 jit_solution(709268878925858497)
XLA Ops:
  0.7 52.4 %attention.1 = bf16[1,16,4096]{2,1,0:T(8,128)(2,1)} custom-call(bf16[1,16,4096]{2,1,0:T(8,128)(2,1)} %q_hbm.1, bf16[1,16,4096]{2,1,0:T(8,128)(2,1)} %k_hbm.1, bf16[1,16,4096]{2,1,0:T(8,128)(2,1)} %v_hbm.1, s32[1]{0:T(128)S(6)} %copy.8.steps_ref, s32[1,256]{1,0:T(1,128)} %history_ref.1, bf16[256,128]{1,0:T(8,128)(2,1)} %gatew_ref.1), custom_call_target="tpu_custom_call" | custom-call | tf_op jit(solution)/shard_map/attention/pallas_call | solution.py:268
  53.0 1.6 %copy.9 = bf16[1,16,4096]{2,1,0:T(8,128)(2,1)} copy(bf16[1,16,4096]{2,1,0:T(8,128)(2,1)} %attention.1) | data formatting | bytes 262144

commit v2 on v0

v2 whole, which is shorter than its diff:
```python
import functools
import math

import jax
import jax.numpy as jnp
from jax import lax
from jax.experimental import pallas as pl
from jax.experimental.pallas import tpu as pltpu
from jax.sharding import PartitionSpec as P

HD = 128
FREQ = 256
RAISE = math.log2(math.e) / math.sqrt(HD)
HIDDEN = -1e30
VLIM = 60
WG = 3
LAG = 1
GN = 4


def places(n_x, n_z, n_g):
    def far(p):
        return (min(p[1], n_z - p[1]), min(p[0], n_x - p[0]))

    every = sorted(((a, b) for a in range(n_x) for b in range(n_z)), key=lambda p: (sum(far(p)), p))
    per = len(every) // n_g
    return every[:per] + sorted(every[per:], key=lambda p: (-far(p)[0], -far(p)[1], p))


def kernel(
    n_span, n_x, n_z, n_g, wrap, tok,
    q_hbm, k_hbm, v_hbm, steps_hbm, history_hbm, gatew_hbm,
    out_ref,
    q_in, k_in, v_in, steps, history, gatew, kv_stage, q_stage, kv, relay, qbuf, obuf, bias, gate_row, top, total, accum,
    in_sem, kv_recv, kv_send, q_recv, q_send, down_send, side_send, wrap_send, relay_recv, relay_send, o_recv, o_send,
):
    n_seq = n_x * n_z
    n_wrap = min(WG, n_g)
    per = n_seq // n_g
    rows = per * tok
    n_chip = n_span // 2
    span, seq, video = lax.axis_index("span"), lax.axis_index("seq"), lax.axis_index("rep")
    chip, core = span // 2, lax.rem(span, 2)
    x, z = seq // n_z, lax.rem(seq, n_z)
    offsets = places(n_x, n_z, n_g)
    x_to = [lax.rem(x + d, n_x) * n_z for d in range(n_x)]
    z_to = [lax.rem(z + d, n_z) for d in range(n_z)]
    ahead = [x_to[a] + z_to[b] for a, b in offsets]
    behind = [x_to[(n_x - a) % n_x] + z_to[(n_z - b) % n_z] for a, b in offsets]
    slots = [(s, s // per, slice(s % per * tok, (s % per + 1) * tok)) for s in range(n_seq)]
    far_first = sorted(
        slots[1:],
        key=lambda s: tuple(-min(d, n - d) for d, n in zip(offsets[s[0]][::-1], (n_z, n_x))),
    )

    fetch = [
        pltpu.make_async_copy(src, dst, in_sem.at[i])
        for i, (src, dst) in enumerate((
            (k_hbm.at[0], k_in), (v_hbm.at[0], v_in), (q_hbm.at[0], q_in),
            (steps_hbm, steps), (history_hbm, history), (gatew_hbm, gatew),
        ))
    ]
    for copy in fetch:
        copy.start()
    barrier = pltpu.get_barrier_semaphore()
    sibling = span + 1 - 2 * core
    last = n_chip - 1
    hop1, hop2 = {"rep": 1 - video, "span": 2 + core}, {"rep": 1 - video, "span": 2 * last + core}

    def greet(to):
        pl.semaphore_signal(barrier, inc=1, device_id=to)

    for s, _, _ in far_first:
        greet({"seq": ahead[s]})
    greet({"span": sibling})
    pl.when(chip > 0)(lambda: greet({"span": span - 2}))
    pl.when(chip < last)(lambda: greet({"span": span + 2}))
    others = n_seq + (chip > 0).astype(jnp.int32) + (chip < last).astype(jnp.int32)
    if wrap:
        pl.when(chip == 0)(lambda: greet(hop1))
        pl.when(chip == 1)(lambda: greet({"rep": 1 - video, "span": core}))
        pl.when(chip == 1)(lambda: greet(hop2))
        pl.when(chip == last)(lambda: greet(hop1))
        others += (chip < 2).astype(jnp.int32) + (chip == 1).astype(jnp.int32) + (chip == last).astype(jnp.int32)

    for copy, inputs, stage in zip(fetch, (k_in, v_in, q_in), (kv_stage.at[:, 0], kv_stage.at[:, 1], q_stage)):
        copy.wait()
        for t in range(n_seq):
            stage[t] = inputs[:, t * HD : (t + 1) * HD]
    kv[span, 0, :, 0:tok, :] = kv_stage[seq]
    qbuf[0:tok, :] = q_stage[seq]
    pl.semaphore_wait(barrier, others)

    for s, g, at in slots[1:]:
        pltpu.make_async_remote_copy(
            src_ref=kv_stage.at[ahead[s]],
            dst_ref=kv.at[span, g, :, at, :],
            send_sem=kv_send,
            recv_sem=kv_recv.at[span, g],
            device_id={"seq": ahead[s]},
        ).start()
    for s, _, _ in far_first:
        pltpu.make_async_remote_copy(
            src_ref=q_stage.at[ahead[s]],
            dst_ref=qbuf.at[s * tok : (s + 1) * tok, :],
            send_sem=q_send,
            recv_sem=q_recv,
            device_id={"seq": ahead[s]},
        ).start()

    for copy in fetch[3:]:
        copy.wait()
    half = FREQ // 2
    k_index = lax.broadcasted_iota(jnp.int32, (8, half), 1).astype(jnp.float32)
    freqs = jnp.exp(-math.log(10000.0) * k_index / half)
    angle = steps[0].astype(jnp.float32) * freqs
    embedding = jnp.concatenate([jnp.cos(angle), jnp.sin(angle)], axis=-1).astype(jnp.bfloat16)
    gate_row[...] = jnp.dot(embedding, gatew[...], preferred_element_type=jnp.float32)

    n_block = n_span * n_seq
    spread = jnp.where(
        lax.broadcasted_iota(jnp.int32, (n_span, n_block), 1) // n_seq
        == lax.broadcasted_iota(jnp.int32, (n_span, n_block), 0),
        history[...],
        0,
    ).astype(jnp.float32).astype(jnp.bfloat16)
    key_slot = lax.broadcasted_iota(jnp.int32, (1, n_seq * tok), 1) // tok
    key_block = jnp.zeros(key_slot.shape, jnp.int32)
    for s in range(n_seq):
        key_block = jnp.where(key_slot == s, behind[s], key_block)
    place = lax.rem(lax.broadcasted_iota(jnp.int32, (n_block, n_seq * tok), 0), n_seq) == key_block
    shown = jnp.dot(
        spread, jnp.where(place, 1.0, 0.0).astype(jnp.bfloat16), preferred_element_type=jnp.float32
    )
    own = lax.broadcasted_iota(jnp.int32, shown.shape, 0) == span
    shade = jnp.where(own | (shown > 0.5), 0.0, HIDDEN)
    for part in range(2):
        bias[part] = shade[:, part * (n_g // 2 * rows) : (part + 1) * (n_g // 2 * rows)]
    top[...] = jnp.full(top.shape, HIDDEN, jnp.float32)
    total[...] = jnp.zeros(total.shape, jnp.float32)
    accum[...] = jnp.zeros(accum.shape, jnp.float32)

    def chunk_copy(j, g, sems, to):
        return pltpu.make_async_remote_copy(
            src_ref=kv.at[j, g],
            dst_ref=kv.at[j, g],
            send_sem=sems.at[j, g],
            recv_sem=kv_recv.at[j, g],
            device_id=to,
        )

    def wrap_copy(g):
        return pltpu.make_async_remote_copy(
            src_ref=kv.at[span, g],
            dst_ref=relay.at[g],
            send_sem=wrap_send.at[g],
            recv_sem=relay_recv.at[g],
            device_id=hop1,
        )

    def relay_copy(g):
        return pltpu.make_async_remote_copy(
            src_ref=relay.at[g],
            dst_ref=kv.at[core, g],
            send_sem=relay_send.at[g],
            recv_sem=kv_recv.at[core, g],
            device_id=hop2,
        )

    def goes_on(h, g):
        if wrap and g < n_wrap:
            return (chip < last) & ((chip < last - 1) | (h < last - 1))
        return chip < last

    def await_chunk(j, g, first=0):
        ref = kv.at[j, g, :, first:rows, :]
        pltpu.make_async_copy(ref, ref, kv_recv.at[j, g]).wait()

    def absorb(j, part):
        mine = pl.ds(part * (n_g // 2), n_g // 2)
        wide = n_g // 2 * rows
        keys = kv[j, mine, 0].reshape(wide, HD)
        values = kv[j, mine, 1].reshape(wide, HD)
        scores = lax.dot_general(
            qbuf[...], keys, (((1,), (1,)), ((), ())), preferred_element_type=jnp.float32
        )
        scores = scores + bias[part, pl.ds(j, 1), :]
        largest = jnp.maximum(jnp.max(scores, axis=-1, keepdims=True), top[...])
        step = min(HD, wide)
        weights = [
            jnp.exp2((scores[:, a : a + step] - largest[:, :step]) * RAISE) for a in range(0, wide, step)
        ]
        added = functools.reduce(jnp.add, weights)
        weights = jnp.concatenate([w.astype(jnp.bfloat16) for w in weights], axis=1)
        summed = jnp.dot(weights, values, preferred_element_type=jnp.float32)
        shrink = jnp.exp2((top[...] - largest) * RAISE)
        total[:, :step] = total[:, :step] * shrink[:, :step] + added
        accum[...] = accum[...] * shrink + summed
        top[...] = largest

    for g in range(n_g):
        if per > 1 or g > 0:
            await_chunk(span, g, tok if g == 0 else 0)
        pl.when(goes_on(0, g))(chunk_copy(span, g, down_send, {"span": span + 2}).start)
        if wrap and g < n_wrap:
            pl.when(chip == 0)(wrap_copy(g).start)
        pl.when(core == 0)(chunk_copy(span, g, side_send, {"span": sibling}).start)

    def take(h, g):
        j = span - 2 * h
        await_chunk(j, g)
        pl.when(goes_on(h, g))(chunk_copy(j, g, down_send, {"span": span + 2}).start)
        chunk_copy(j, g, side_send, {"span": sibling}).start()

    for g in range(n_g + LAG):
        if g < n_g:
            pl.when(chip >= 1)(functools.partial(take, 1, g))
        if wrap and 0 <= g - LAG < n_wrap:

            @pl.when(chip == 1)
            def _():
                here = relay.at[g - LAG]
                pltpu.make_async_copy(here, here, relay_recv.at[g - LAG]).wait()
                relay_copy(g - LAG).start()

    q_rest = q_stage.at[1:n_seq]
    pltpu.make_async_copy(q_rest, q_rest, q_recv).wait()

    @pl.loop(0, chip + 1)
    def _(h):
        @pl.loop(0, 2)
        def _(part):
            @pl.when(h > 1)
            def _():
                for g in range(n_g):
                    pl.when(part == g // (n_g // 2))(functools.partial(take, h, g))

            @pl.loop(0, jnp.where((h > 0) | (core == 1), 2, 1))
            def _(side):
                j = jnp.where(side == 1, sibling, span) - 2 * h

                @pl.when(side == 1)
                def _():
                    for g in range(n_g // 2):
                        await_chunk(j, part * (n_g // 2) + g)

                absorb(j, part)

    for g in list(range(1, n_g)) + [0]:
        at = slice(g * rows, (g + 1) * rows)
        whole = jnp.sum(total[at, : min(HD, n_g // 2 * rows)], axis=-1, keepdims=True)
        obuf[at, :] = (accum[at, :] / whole * gate_row[0:1, :]).astype(jnp.bfloat16)
        for s, _, _ in far_first:
            if s // per == g:
                pltpu.make_async_remote_copy(
                    src_ref=obuf.at[s * tok : (s + 1) * tok, :],
                    dst_ref=out_ref.at[0, :, pl.ds(pl.multiple_of(seq * HD, HD), HD)],
                    send_sem=o_send,
                    recv_sem=o_recv,
                    device_id={"seq": behind[s]},
                ).start()
    out_ref[0, :, pl.ds(pl.multiple_of(seq * HD, HD), HD)] = obuf[0:tok, :]

    def drain(ref, sem):
        pltpu.make_async_copy(ref, ref, sem).wait()

    drain(kv_stage.at[1:n_seq], kv_send)
    drain(q_stage.at[1:n_seq], q_send)
    for h in range(n_chip):

        @pl.when(chip >= h)
        def _():
            for g in range(n_g):
                pl.when(goes_on(h, g))(chunk_copy(span - 2 * h, g, down_send, {"span": span + 2}).wait_send)

        @pl.when((chip >= h) & ((core == 0) | (h > 0)))
        def _():
            for g in range(n_g):
                chunk_copy(span - 2 * h, g, side_send, {"span": sibling}).wait_send()

    if wrap:
        for g in range(n_wrap):
            pl.when(chip == 0)(wrap_copy(g).wait_send)
            pl.when(chip == 1)(relay_copy(g).wait_send)
    drain(obuf.at[tok:, :], o_send)
    drain(out_ref.at[0, :, 0 : (n_seq - 1) * HD], o_recv)


def body(queries, keys, values, timesteps, history, gate_weight):
    n_span, n_seq = lax.axis_size("span"), lax.axis_size("seq")
    n_x = 4 if n_seq == 32 else 2
    n_z = n_seq // n_x
    n_g = GN if n_seq == 32 else 2
    wrap = n_span == 8 and lax.axis_size("rep") == 2
    tok, width = queries.shape[1], queries.shape[2]
    bf16, f32 = jnp.bfloat16, jnp.float32
    rows = n_seq // n_g * tok
    whole = n_seq * tok
    return pl.pallas_call(
        functools.partial(kernel, n_span, n_x, n_z, n_g, wrap, tok),
        out_shape=jax.ShapeDtypeStruct(queries.shape, bf16),
        in_specs=[pl.BlockSpec(memory_space=pltpu.HBM)] * 6,
        out_specs=pl.BlockSpec(memory_space=pltpu.VMEM),
        scratch_shapes=[
            pltpu.VMEM((tok, width), bf16),
            pltpu.VMEM((tok, width), bf16),
            pltpu.VMEM((tok, width), bf16),
            pltpu.SMEM(timesteps.shape, timesteps.dtype),
            pltpu.VMEM(history.shape, history.dtype),
            pltpu.VMEM(gate_weight.shape, bf16),
            pltpu.VMEM((n_seq, 2, tok, HD), bf16),
            pltpu.VMEM((n_seq, tok, HD), bf16),
            pltpu.VMEM((n_span, n_g, 2, rows, HD), bf16),
            pltpu.VMEM((n_g, 2, rows, HD), bf16),
            pltpu.VMEM((whole, HD), bf16),
            pltpu.VMEM((whole, HD), bf16),
            pltpu.VMEM((2, n_span, whole // 2), f32),
            pltpu.VMEM((8, HD), f32),
            pltpu.VMEM((whole, HD), f32),
            pltpu.VMEM((whole, HD), f32),
            pltpu.VMEM((whole, HD), f32),
            pltpu.SemaphoreType.DMA((6,)),
            pltpu.SemaphoreType.DMA((n_span, n_g)),
            pltpu.SemaphoreType.DMA,
            pltpu.SemaphoreType.DMA,
            pltpu.SemaphoreType.DMA,
            pltpu.SemaphoreType.DMA((n_span, n_g)),
            pltpu.SemaphoreType.DMA((n_span, n_g)),
            pltpu.SemaphoreType.DMA((n_g,)),
            pltpu.SemaphoreType.DMA((n_g,)),
            pltpu.SemaphoreType.DMA((n_g,)),
            pltpu.SemaphoreType.DMA,
            pltpu.SemaphoreType.DMA,
        ],
        compiler_params=pltpu.CompilerParams(
            collective_id=0, has_side_effects=True, vmem_limit_bytes=VLIM * 2**20
        ),
        name="attention",
    )(queries, keys, values, timesteps, history, gate_weight)


def solution(mesh):
    return jax.shard_map(
        body,
        mesh=mesh,
        in_specs=(
            P(("rep", "span"), "seq", None),
            P(("rep", "span"), "seq", None),
            P(("rep", "span"), "seq", None),
            P(("rep", "span")),
            P(("rep", "span"), None),
            P(None, "seq"),
        ),
        out_specs=P(("rep", "span"), "seq", None),
        check_vma=False,
    )
```

time: 265 us -> 49.3 us (0.19)
  the two profiles are of different devices: /device:TPU:57 before, /device:TPU:56 now
where the time goes in v2:
time: 49.3 us; the launch traced here: 49.1 us
  Pallas kernels  46.9 us (95%)
  local copies, waits for them, and re-layouts  1.57 us (3%)
  between operations  0.66 us (1%)
    pallas_call x1, Pallas kernels, body(): pl.pallas_call(functools.partial(kernel, n_span, n_x, n_z, n_g, wrap, tok...  46.9 us
    unnamed x1, local copies, waits for them, and re-layouts  1.57 us

profile of v2, /device:TPU:56, one launch (start us, length us, event | category | flops | bytes accessed | tf_op | source)
XLA Modules:
  0.0 49.1 jit_solution(177444722564615860)
XLA Ops:
  0.7 46.9 %attention.1 = bf16[1,16,4096]{2,1,0:T(8,128)(2,1)} custom-call(bf16[1,16,4096]{2,1,0:T(8,128)(2,1)} %q_hbm.1, bf16[1,16,4096]{2,1,0:T(8,128)(2,1)} %k_hbm.1, bf16[1,16,4096]{2,1,0:T(8,128)(2,1)} %v_hbm.1, s32[1]{0:T(128)S(6)} %copy.8.steps_hbm, s32[1,256]{1,0:T(1,128)} %history_hbm.1, bf16[256,128]{1,0:T(8,128)(2,1)} %gatew_hbm.1), custom_call_target="tpu_custom_call" | custom-call | tf_op jit(solution)/shard_map/attention/pallas_call | solution.py:299
  47.6 1.6 %copy.9 = bf16[1,16,4096]{2,1,0:T(8,128)(2,1)} copy(bf16[1,16,4096]{2,1,0:T(8,128)(2,1)} %attention.1) | data formatting | bytes 262144

commit v3 on v2

--- a/solution.py
+++ b/solution.py
@@ -14,7 +14,6 @@
 HIDDEN = -1e30
 VLIM = 60
 WG = 3
-LAG = 1
 GN = 4
 
 
@@ -35,7 +34,7 @@
     in_sem, kv_recv, kv_send, q_recv, q_send, down_send, side_send, wrap_send, relay_recv, relay_send, o_recv, o_send,
 ):
     n_seq = n_x * n_z
-    n_wrap = min(WG, n_g)
+    n_wrap = min(WG, n_g) if wrap else 0
     per = n_seq // n_g
     rows = per * tok
     n_chip = n_span // 2
@@ -77,26 +76,28 @@
     pl.when(chip < last)(lambda: greet({"span": span + 2}))
     others = n_seq + (chip > 0).astype(jnp.int32) + (chip < last).astype(jnp.int32)
     if wrap:
+        pl.when(chip == 0)(lambda: greet({"span": span + 2 * last}))
+        pl.when(chip == last)(lambda: greet({"span": core}))
         pl.when(chip == 0)(lambda: greet(hop1))
         pl.when(chip == 1)(lambda: greet({"rep": 1 - video, "span": core}))
         pl.when(chip == 1)(lambda: greet(hop2))
         pl.when(chip == last)(lambda: greet(hop1))
-        others += (chip < 2).astype(jnp.int32) + (chip == 1).astype(jnp.int32) + (chip == last).astype(jnp.int32)
+        others += 2 * (1 - ((chip > 1) & (chip < last)).astype(jnp.int32))
 
     for copy, inputs, stage in zip(fetch, (k_in, v_in, q_in), (kv_stage.at[:, 0], kv_stage.at[:, 1], q_stage)):
         copy.wait()
         for t in range(n_seq):
             stage[t] = inputs[:, t * HD : (t + 1) * HD]
-    kv[span, 0, :, 0:tok, :] = kv_stage[seq]
+    kv[span * n_g, :, 0:tok, :] = kv_stage[seq]
     qbuf[0:tok, :] = q_stage[seq]
     pl.semaphore_wait(barrier, others)
 
     for s, g, at in slots[1:]:
         pltpu.make_async_remote_copy(
             src_ref=kv_stage.at[ahead[s]],
-            dst_ref=kv.at[span, g, :, at, :],
+            dst_ref=kv.at[span * n_g + g, :, at, :],
             send_sem=kv_send,
-            recv_sem=kv_recv.at[span, g],
+            recv_sem=kv_recv.at[span * n_g + g],
             device_id={"seq": ahead[s]},
         ).start()
     for s, _, _ in far_first:
@@ -110,9 +111,9 @@
 
     for copy in fetch[3:]:
         copy.wait()
-    half = FREQ // 2
-    k_index = lax.broadcasted_iota(jnp.int32, (8, half), 1).astype(jnp.float32)
-    freqs = jnp.exp(-math.log(10000.0) * k_index / half)
+    n_freq = FREQ // 2
+    k_index = lax.broadcasted_iota(jnp.int32, (8, n_freq), 1).astype(jnp.float32)
+    freqs = jnp.exp(-math.log(10000.0) * k_index / n_freq)
     angle = steps[0].astype(jnp.float32) * freqs
     embedding = jnp.concatenate([jnp.cos(angle), jnp.sin(angle)], axis=-1).astype(jnp.bfloat16)
     gate_row[...] = jnp.dot(embedding, gatew[...], preferred_element_type=jnp.float32)
@@ -142,18 +143,18 @@
 
     def chunk_copy(j, g, sems, to):
         return pltpu.make_async_remote_copy(
-            src_ref=kv.at[j, g],
-            dst_ref=kv.at[j, g],
-            send_sem=sems.at[j, g],
-            recv_sem=kv_recv.at[j, g],
+            src_ref=kv.at[j * n_g + g],
+            dst_ref=kv.at[j * n_g + g],
+            send_sem=sems,
+            recv_sem=kv_recv.at[j * n_g + g],
             device_id=to,
         )
 
     def wrap_copy(g):
         return pltpu.make_async_remote_copy(
-            src_ref=kv.at[span, g],
+            src_ref=kv.at[span * n_g + g],
             dst_ref=relay.at[g],
-            send_sem=wrap_send.at[g],
+            send_sem=wrap_send,
             recv_sem=relay_recv.at[g],
             device_id=hop1,
         )
@@ -161,38 +162,43 @@
     def relay_copy(g):
         return pltpu.make_async_remote_copy(
             src_ref=relay.at[g],
-            dst_ref=kv.at[core, g],
-            send_sem=relay_send.at[g],
-            recv_sem=kv_recv.at[core, g],
+            dst_ref=kv.at[core * n_g + g],
+            send_sem=relay_send,
+            recv_sem=kv_recv.at[core * n_g + g],
             device_id=hop2,
         )
 
-    def goes_on(h, g):
-        if wrap and g < n_wrap:
-            return (chip < last) & ((chip < last - 1) | (h < last - 1))
+    def goes_on(h):
+        if wrap and h == last - 1:
+            return chip < 0
         return chip < last
 
     def await_chunk(j, g, first=0):
-        ref = kv.at[j, g, :, first:rows, :]
-        pltpu.make_async_copy(ref, ref, kv_recv.at[j, g]).wait()
-
-    def absorb(j, part):
-        mine = pl.ds(part * (n_g // 2), n_g // 2)
-        wide = n_g // 2 * rows
-        keys = kv[j, mine, 0].reshape(wide, HD)
-        values = kv[j, mine, 1].reshape(wide, HD)
+        ref = kv.at[j * n_g + g, :, first:rows, :]
+        pltpu.make_async_copy(ref, ref, kv_recv.at[j * n_g + g]).wait()
+
+    half = n_g // 2
+
+    def absorb(*pieces):
+        wide = half * rows
+        keys, values, shade = [], [], []
+        for j, part in pieces:
+            mine = pl.ds(j * n_g + part * half, half)
+            keys.append(kv[mine, 0].reshape(wide, HD))
+            values.append(kv[mine, 1].reshape(wide, HD))
+            shade.append(bias[part, pl.ds(j, 1), :])
         scores = lax.dot_general(
-            qbuf[...], keys, (((1,), (1,)), ((), ())), preferred_element_type=jnp.float32
-        )
-        scores = scores + bias[part, pl.ds(j, 1), :]
+            qbuf[...], jnp.concatenate(keys), (((1,), (1,)), ((), ())), preferred_element_type=jnp.float32
+        )
+        scores = scores + jnp.concatenate(shade, axis=1)
         largest = jnp.maximum(jnp.max(scores, axis=-1, keepdims=True), top[...])
-        step = min(HD, wide)
+        step = min(HD, 2 * wide)
         weights = [
-            jnp.exp2((scores[:, a : a + step] - largest[:, :step]) * RAISE) for a in range(0, wide, step)
+            jnp.exp2((scores[:, a : a + step] - largest[:, :step]) * RAISE) for a in range(0, 2 * wide, step)
         ]
         added = functools.reduce(jnp.add, weights)
         weights = jnp.concatenate([w.astype(jnp.bfloat16) for w in weights], axis=1)
-        summed = jnp.dot(weights, values, preferred_element_type=jnp.float32)
+        summed = jnp.dot(weights, jnp.concatenate(values), preferred_element_type=jnp.float32)
         shrink = jnp.exp2((top[...] - largest) * RAISE)
         total[:, :step] = total[:, :step] * shrink[:, :step] + added
         accum[...] = accum[...] * shrink + summed
@@ -201,54 +207,92 @@
     for g in range(n_g):
         if per > 1 or g > 0:
             await_chunk(span, g, tok if g == 0 else 0)
-        pl.when(goes_on(0, g))(chunk_copy(span, g, down_send, {"span": span + 2}).start)
-        if wrap and g < n_wrap:
-            pl.when(chip == 0)(wrap_copy(g).start)
+        pl.when(goes_on(0))(chunk_copy(span, g, down_send, {"span": span + 2}).start)
+        if wrap:
+            far = wrap_copy(g) if g < n_wrap else chunk_copy(span, g, down_send, {"span": span + 2 * last})
+            pl.when(chip == 0)(far.start)
         pl.when(core == 0)(chunk_copy(span, g, side_send, {"span": sibling}).start)
 
     def take(h, g):
         j = span - 2 * h
         await_chunk(j, g)
-        pl.when(goes_on(h, g))(chunk_copy(j, g, down_send, {"span": span + 2}).start)
+        pl.when(goes_on(h))(chunk_copy(j, g, down_send, {"span": span + 2}).start)
         chunk_copy(j, g, side_send, {"span": sibling}).start()
 
-    for g in range(n_g + LAG):
-        if g < n_g:
-            pl.when(chip >= 1)(functools.partial(take, 1, g))
-        if wrap and 0 <= g - LAG < n_wrap:
-
-            @pl.when(chip == 1)
-            def _():
-                here = relay.at[g - LAG]
-                pltpu.make_async_copy(here, here, relay_recv.at[g - LAG]).wait()
-                relay_copy(g - LAG).start()
-
+    def halves(part):
+        return range(part * n_g // 2, (part + 1) * n_g // 2)
+
+    def order(c):
+        if wrap and c == last and c == 3:
+            return [(1, 0), (1, 1), (2, 0), (3, 0), (2, 1), (3, 1)]
+        return [(h, part) for h in range(1, c + 1) for part in range(2)]
+
+    def passes(c):
+        halves_in = order(c)
+        if c == 0:
+            return {}
+        if wrap and c == 1:
+            return {-1: [(1, 0)], 0: [0, (1, 1), 1], 1: [2, 3]}
+        if c < last:
+            ahead_of = {-1: [(1, 0), (1, 1)]}
+            rest = halves_in[2:]
+        else:
+            ahead_of = {-1: [(1, 0)]}
+            rest = halves_in[1:]
+        for n, one in enumerate(rest):
+            ahead_of[n] = [one]
+        return ahead_of
+
+    def pass_through(what):
+        for one in what:
+            if isinstance(one, tuple):
+                for g in halves(one[1]):
+                    take(one[0], g)
+            elif one < n_wrap:
+                here = relay.at[one]
+                pltpu.make_async_copy(here, here, relay_recv.at[one]).wait()
+                relay_copy(one).start()
+
+    for c in range(n_chip):
+        if passes(c).get(-1):
+            pl.when(chip == c)(functools.partial(pass_through, passes(c)[-1]))
     q_rest = q_stage.at[1:n_seq]
     pltpu.make_async_copy(q_rest, q_rest, q_recv).wait()
 
-    @pl.loop(0, chip + 1)
-    def _(h):
-        @pl.loop(0, 2)
-        def _(part):
-            @pl.when(h > 1)
-            def _():
-                for g in range(n_g):
-                    pl.when(part == g // (n_g // 2))(functools.partial(take, h, g))
-
-            @pl.loop(0, jnp.where((h > 0) | (core == 1), 2, 1))
-            def _(side):
-                j = jnp.where(side == 1, sibling, span) - 2 * h
-
-                @pl.when(side == 1)
-                def _():
-                    for g in range(n_g // 2):
-                        await_chunk(j, part * (n_g // 2) + g)
-
-                absorb(j, part)
+    @pl.loop(0, 2 * chip + core + 1)
+    def _(i):
+        k = i - (1 + core)
+        here = k < 0
+        h, part = (k + 2) // 2, lax.rem(k + 2, 2)
+        if order(last) != [(m // 2 + 1, m % 2) for m in range(2 * last)]:
+            for m, (hop, which) in enumerate(order(last)):
+                h = jnp.where((chip == last) & (k == m), hop, h)
+                part = jnp.where((chip == last) & (k == m), which, part)
+        up, side = span - 2 * h, sibling - 2 * h
+        for c in range(n_chip):
+            for when, what in passes(c).items():
+                if when >= 0:
+                    pl.when((chip == c) & (k == when))(functools.partial(pass_through, what))
+
+        @pl.when(jnp.logical_not(here))
+        def _():
+            for g in range(half):
+                await_chunk(side, part * half + g)
+
+        @pl.when(here & (i == 1))
+        def _():
+            for g in range(n_g):
+                await_chunk(sibling, g)
+
+        only = jnp.where(i == 1, sibling, span)
+        absorb(
+            (jnp.where(here, only, up), jnp.where(here, 0, part)),
+            (jnp.where(here, only, side), jnp.where(here, 1, part)),
+        )
 
     for g in list(range(1, n_g)) + [0]:
         at = slice(g * rows, (g + 1) * rows)
-        whole = jnp.sum(total[at, : min(HD, n_g // 2 * rows)], axis=-1, keepdims=True)
+        whole = jnp.sum(total[at, : min(HD, n_g * rows)], axis=-1, keepdims=True)
         obuf[at, :] = (accum[at, :] / whole * gate_row[0:1, :]).astype(jnp.bfloat16)
         for s, _, _ in far_first:
             if s // per == g:
@@ -259,29 +303,28 @@
                     recv_sem=o_recv,
                     device_id={"seq": behind[s]},
                 ).start()
-    out_ref[0, :, pl.ds(pl.multiple_of(seq * HD, HD), HD)] = obuf[0:tok, :]
+    mine = pltpu.make_async_copy(
+        obuf.at[0:tok, :], out_ref.at[0, :, pl.ds(pl.multiple_of(seq * HD, HD), HD)], in_sem.at[0]
+    )
+    mine.start()
+    mine.wait()
 
     def drain(ref, sem):
         pltpu.make_async_copy(ref, ref, sem).wait()
 
     drain(kv_stage.at[1:n_seq], kv_send)
     drain(q_stage.at[1:n_seq], q_send)
-    for h in range(n_chip):
-
-        @pl.when(chip >= h)
-        def _():
-            for g in range(n_g):
-                pl.when(goes_on(h, g))(chunk_copy(span - 2 * h, g, down_send, {"span": span + 2}).wait_send)
-
-        @pl.when((chip >= h) & ((core == 0) | (h > 0)))
-        def _():
-            for g in range(n_g):
-                chunk_copy(span - 2 * h, g, side_send, {"span": sibling}).wait_send()
-
-    if wrap:
-        for g in range(n_wrap):
-            pl.when(chip == 0)(wrap_copy(g).wait_send)
-            pl.when(chip == 1)(relay_copy(g).wait_send)
+    for c in range(n_chip):
+        passed = [h for h in range(c + 1) if not (wrap and h == last - 1)] if c < last else []
+        n_down = len(passed) * n_g + (n_g - n_wrap if wrap and c == 0 else 0)
+        if n_down:
+            pl.when(chip == c)(functools.partial(drain, kv.at[0:n_down], down_send))
+        pl.when((chip == c) & (core == 0))(functools.partial(drain, kv.at[0 : (c + 1) * n_g], side_send))
+        if c > 0:
+            pl.when((chip == c) & (core == 1))(functools.partial(drain, kv.at[0 : c * n_g], side_send))
+    if n_wrap:
+        pl.when(chip == 0)(functools.partial(drain, relay.at[0:n_wrap], wrap_send))
+        pl.when(chip == 1)(functools.partial(drain, relay.at[0:n_wrap], relay_send))
     drain(obuf.at[tok:, :], o_send)
     drain(out_ref.at[0, :, 0 : (n_seq - 1) * HD], o_recv)
 
@@ -298,7 +341,7 @@
     whole = n_seq * tok
     return pl.pallas_call(
         functools.partial(kernel, n_span, n_x, n_z, n_g, wrap, tok),
-        out_shape=jax.ShapeDtypeStruct(queries.shape, bf16),
+        out_shape=pltpu.VMEM(queries.shape, bf16),
         in_specs=[pl.BlockSpec(memory_space=pltpu.HBM)] * 6,
         out_specs=pl.BlockSpec(memory_space=pltpu.VMEM),
         scratch_shapes=[
@@ -310,7 +353,7 @@
             pltpu.VMEM(gate_weight.shape, bf16),
             pltpu.VMEM((n_seq, 2, tok, HD), bf16),
             pltpu.VMEM((n_seq, tok, HD), bf16),
-            pltpu.VMEM((n_span, n_g, 2, rows, HD), bf16),
+            pltpu.VMEM((n_span * n_g, 2, rows, HD), bf16),
             pltpu.VMEM((n_g, 2, rows, HD), bf16),
             pltpu.VMEM((whole, HD), bf16),
             pltpu.VMEM((whole, HD), bf16),
@@ -320,15 +363,15 @@
             pltpu.VMEM((whole, HD), f32),
             pltpu.VMEM((whole, HD), f32),
             pltpu.SemaphoreType.DMA((6,)),
-            pltpu.SemaphoreType.DMA((n_span, n_g)),
-            pltpu.SemaphoreType.DMA,
-            pltpu.SemaphoreType.DMA,
-            pltpu.SemaphoreType.DMA,
-            pltpu.SemaphoreType.DMA((n_span, n_g)),
-            pltpu.SemaphoreType.DMA((n_span, n_g)),
+            pltpu.SemaphoreType.DMA((n_span * n_g,)),
+            pltpu.SemaphoreType.DMA,
+            pltpu.SemaphoreType.DMA,
+            pltpu.SemaphoreType.DMA,
+            pltpu.SemaphoreType.DMA,
+            pltpu.SemaphoreType.DMA,
+            pltpu.SemaphoreType.DMA,
             pltpu.SemaphoreType.DMA((n_g,)),
-            pltpu.SemaphoreType.DMA((n_g,)),
-            pltpu.SemaphoreType.DMA((n_g,)),
+            pltpu.SemaphoreType.DMA,
             pltpu.SemaphoreType.DMA,
             pltpu.SemaphoreType.DMA,
         ],

time: 49.3 us -> 45.2 us (0.917)
  Pallas kernels: 46.9 us -> 43.4 us
  local copies, waits for them, and re-layouts: 1.57 us -> 0.66 us
    pallas_call x1, Pallas kernels: 46.9 us -> 43.4 us  [body(): pl.pallas_call(functools.partial(kernel, n_span, n_x, n_z, n_g, wrap, tok...]
    unnamed x1, local copies, waits for them, and re-layouts: 1.57 us -> 0.66 us
where the time goes in v3:
time: 45.2 us; the launch traced here: 44.8 us
  Pallas kernels  43.4 us (96%)
  local copies, waits for them, and re-layouts  0.66 us (1%)
  between operations  0.66 us (1%)
    pallas_call x1, Pallas kernels, body(): pl.pallas_call(functools.partial(kernel, n_span, n_x, n_z, n_g, wrap, tok...  43.4 us

profile of v3, /device:TPU:56, one launch (start us, length us, event | category | flops | bytes accessed | tf_op | source)
XLA Modules:
  0.0 44.8 jit_solution(12014761595259647664)
XLA Ops:
  0.7 43.4 %attention.1 = bf16[1,16,4096]{2,1,0:T(8,128)(2,1)S(1)} custom-call(bf16[1,16,4096]{2,1,0:T(8,128)(2,1)} %q_hbm.1, bf16[1,16,4096]{2,1,0:T(8,128)(2,1)} %k_hbm.1, bf16[1,16,4096]{2,1,0:T(8,128)(2,1)} %v_hbm.1, s32[1]{0:T(128)S(6)} %copy.9.steps_hbm, s32[1,256]{1,0:T(1,128)} %history_hbm.1, bf16[256,128]{1,0:T(8,128)(2,1)} %gatew_hbm.1), custom_call_target="tpu_custom_call" | custom-call | tf_op jit(solution)/shard_map/attention/pallas_call | solution.py:342
  44.1 0.7 %copy.8 = bf16[1,16,4096]{2,1,0:T(8,128)(2,1)} copy(bf16[1,16,4096]{2,1,0:T(8,128)(2,1)S(1)} %attention.1) | data formatting | bytes 262144

commit v4 on v3

--- a/solution.py
+++ b/solution.py
@@ -21,9 +21,13 @@
     def far(p):
         return (min(p[1], n_z - p[1]), min(p[0], n_x - p[0]))
 
-    every = sorted(((a, b) for a in range(n_x) for b in range(n_z)), key=lambda p: (sum(far(p)), p))
+    def far_first(p):
+        return (-far(p)[0], -far(p)[1], p)
+
+    every = sorted(((a, b) for a in range(n_x) for b in range(n_z)), key=lambda p: (far(p), p))
     per = len(every) // n_g
-    return every[:per] + sorted(every[per:], key=lambda p: (-far(p)[0], -far(p)[1], p))
+    rest = sorted(every[per:], key=lambda p: (sum(far(p)), p))
+    return every[:per] + sorted(rest[:per], key=far_first) + sorted(rest[per:], key=far_first)
 
 
 def kernel(
@@ -31,10 +35,11 @@
     q_hbm, k_hbm, v_hbm, steps_hbm, history_hbm, gatew_hbm,
     out_ref,
     q_in, k_in, v_in, steps, history, gatew, kv_stage, q_stage, kv, relay, qbuf, obuf, bias, gate_row, top, total, accum,
-    in_sem, kv_recv, kv_send, q_recv, q_send, down_send, side_send, wrap_send, relay_recv, relay_send, o_recv, o_send,
+    in_sem, kv_recv, kv_send, direct_send, q_recv, q_send, down_send, side_send, wrap_send, relay_recv, relay_send, o_recv, o_send,
 ):
     n_seq = n_x * n_z
     n_wrap = min(WG, n_g) if wrap else 0
+    n_direct = 1
     per = n_seq // n_g
     rows = per * tok
     n_chip = n_span // 2
@@ -74,7 +79,16 @@
     greet({"span": sibling})
     pl.when(chip > 0)(lambda: greet({"span": span - 2}))
     pl.when(chip < last)(lambda: greet({"span": span + 2}))
-    others = n_seq + (chip > 0).astype(jnp.int32) + (chip < last).astype(jnp.int32)
+    near = slots[:per]
+
+    def greet_near(to):
+        for s, _, _ in near[1:]:
+            greet({**to, "seq": behind[s]})
+
+    others = n_seq
+    pl.when(chip > 0)(lambda: greet_near({"span": span - 2}))
+    others += (per - 1) * (chip < last).astype(jnp.int32)
+    others += (chip > 0).astype(jnp.int32) + (chip < last).astype(jnp.int32)
     if wrap:
         pl.when(chip == 0)(lambda: greet({"span": span + 2 * last}))
         pl.when(chip == last)(lambda: greet({"span": core}))
@@ -92,6 +106,17 @@
     qbuf[0:tok, :] = q_stage[seq]
     pl.semaphore_wait(barrier, others)
 
+    def send_near():
+        for s, g, at in near:
+            pltpu.make_async_remote_copy(
+                src_ref=kv_stage.at[ahead[s]],
+                dst_ref=kv.at[span * n_g + g, :, at, :],
+                send_sem=direct_send,
+                recv_sem=kv_recv.at[span * n_g + g],
+                device_id={"span": span + 2, "seq": ahead[s]},
+            ).start()
+
+    pl.when(chip < last)(send_near)
     for s, g, at in slots[1:]:
         pltpu.make_async_remote_copy(
             src_ref=kv_stage.at[ahead[s]],
@@ -114,7 +139,7 @@
     n_freq = FREQ // 2
     k_index = lax.broadcasted_iota(jnp.int32, (8, n_freq), 1).astype(jnp.float32)
     freqs = jnp.exp(-math.log(10000.0) * k_index / n_freq)
-    angle = steps[0].astype(jnp.float32) * freqs
+    angle = steps[...].astype(jnp.float32) * freqs
     embedding = jnp.concatenate([jnp.cos(angle), jnp.sin(angle)], axis=-1).astype(jnp.bfloat16)
     gate_row[...] = jnp.dot(embedding, gatew[...], preferred_element_type=jnp.float32)
 
@@ -204,96 +229,121 @@
         accum[...] = accum[...] * shrink + summed
         top[...] = largest
 
-    for g in range(n_g):
-        if per > 1 or g > 0:
-            await_chunk(span, g, tok if g == 0 else 0)
-        pl.when(goes_on(0))(chunk_copy(span, g, down_send, {"span": span + 2}).start)
-        if wrap:
-            far = wrap_copy(g) if g < n_wrap else chunk_copy(span, g, down_send, {"span": span + 2 * last})
-            pl.when(chip == 0)(far.start)
-        pl.when(core == 0)(chunk_copy(span, g, side_send, {"span": sibling}).start)
-
     def take(h, g):
         j = span - 2 * h
         await_chunk(j, g)
         pl.when(goes_on(h))(chunk_copy(j, g, down_send, {"span": span + 2}).start)
         chunk_copy(j, g, side_send, {"span": sibling}).start()
 
+    pl.when(chip > 0)(functools.partial(take, 1, 0))
+    for g in range(n_g):
+        if per > 1 or g > 0:
+            await_chunk(span, g, tok if g == 0 else 0)
+        if g >= n_direct:
+            pl.when(goes_on(0))(chunk_copy(span, g, down_send, {"span": span + 2}).start)
+        if g < n_wrap:
+            pl.when(chip == 0)(wrap_copy(g).start)
+        pl.when(core == 0)(chunk_copy(span, g, side_send, {"span": sibling}).start)
+
     def halves(part):
-        return range(part * n_g // 2, (part + 1) * n_g // 2)
-
-    def order(c):
-        if wrap and c == last and c == 3:
-            return [(1, 0), (1, 1), (2, 0), (3, 0), (2, 1), (3, 1)]
-        return [(h, part) for h in range(1, c + 1) for part in range(2)]
-
-    def passes(c):
-        halves_in = order(c)
+        return range(part * half, (part + 1) * half)
+
+    def do(op, *what):
+        if op == "take":
+            for g in halves(what[1]):
+                if what[0] > 1 or g >= n_direct:
+                    take(what[0], g)
+        elif op == "side":
+            for g in halves(what[1]):
+                await_chunk(sibling - 2 * what[0], g)
+        elif op == "relay":
+            if what[0] < n_wrap:
+                here = relay.at[what[0]]
+                pltpu.make_async_copy(here, here, relay_recv.at[what[0]]).wait()
+                relay_copy(what[0]).start()
+        elif op == "far":
+            for g in range(n_wrap, n_g) if wrap else []:
+                chunk_copy(span, g, down_send, {"span": span + 2 * last}).start()
+        elif op == "queries":
+            rest = q_stage.at[1:n_seq]
+            pltpu.make_async_copy(rest, rest, q_recv).wait()
+
+    def plan(c, k):
+        def take_both(h):
+            return [("take", h, 0), ("take", h, 1)]
+
+        def side_both(h):
+            return [("side", h, 0), ("side", h, 1)]
+
+        def whole(d):
+            return [((d, 0), (d, 1))]
+
+        def up(h):
+            return whole(-2 * h)
+
+        def side(h):
+            return side_both(h) + whole(1 - 2 * k - 2 * h)
+
+        def both_up(part):
+            return [((-2 * (last - 1), part), (-2 * last, part))]
+
+        def both_side(part):
+            d = 1 - 2 * k
+            return [("side", last - 1, part), ("side", last, part), ((d - 2 * (last - 1), part), (d - 2 * last, part))]
+
+        start = [("queries",)] + whole(0)
+        relays = [[("relay", g)] for g in range(n_g)] + [[]] * 4
         if c == 0:
-            return {}
-        if wrap and c == 1:
-            return {-1: [(1, 0)], 0: [0, (1, 1), 1], 1: [2, 3]}
-        if c < last:
-            ahead_of = {-1: [(1, 0), (1, 1)]}
-            rest = halves_in[2:]
-        else:
-            ahead_of = {-1: [(1, 0)]}
-            rest = halves_in[1:]
-        for n, one in enumerate(rest):
-            ahead_of[n] = [one]
-        return ahead_of
-
-    def pass_through(what):
-        for one in what:
-            if isinstance(one, tuple):
-                for g in halves(one[1]):
-                    take(one[0], g)
-            elif one < n_wrap:
-                here = relay.at[one]
-                pltpu.make_async_copy(here, here, relay_recv.at[one]).wait()
-                relay_copy(one).start()
+            return start[:1] + [("far",)] + start[1:] + (side(0) if k == 1 else [])
+        if c == 1 and k == 0:
+            return ([("take", 1, 0)] + start + relays[0] + [("take", 1, 1)] + relays[1] + side(1) + relays[2] + relays[3]
+                    + up(1))
+        if c == 1:
+            return (take_both(1) + start + relays[0] + up(1) + relays[1] + side(0) + relays[2] + relays[3] + side(1))
+        if c == 2 and k == 0:
+            return ([("take", 1, 0)] + start + side(1) + [("take", 1, 1)] + up(1) + side(2) + take_both(2) + up(2))
+        if c == 2:
+            return take_both(1) + start + up(1) + side(0) + take_both(2) + up(2) + side(1) + side(2)
+        if k == 0:
+            return ([("take", 1, 0)] + start + side(1) + [("take", 1, 1)] + up(1)
+                    + [("take", 2, 0)] + side(2) + [("take", 3, 0)] + both_up(0)
+                    + [("take", 2, 1), ("take", 3, 1)] + side(3)
+                    + both_up(1))
+        return (take_both(1) + start + up(1) + side(0) + take_both(2) + up(2) + side(1) + take_both(3) + up(3)
+                + both_side(0) + both_side(1))
+
+    def run(c, k):
+        steps, waits = [], []
+        for one in plan(c, k):
+            if isinstance(one[0], str):
+                waits.append(one)
+            else:
+                steps.append((waits, one))
+                waits = []
+
+        @pl.loop(0, len(steps))
+        def _(i):
+            pieces = [[jnp.int32(0), jnp.int32(0)], [jnp.int32(0), jnp.int32(0)]]
+            for n, (waits, pair) in enumerate(steps):
+
+                @pl.when(i == n)
+                def _():
+                    for one in waits:
+                        do(*one)
+
+                for piece, (distance, part) in zip(pieces, pair):
+                    piece[0] = jnp.where(i == n, distance, piece[0])
+                    piece[1] = jnp.where(i == n, part, piece[1])
+            absorb(*((span + distance, part) for distance, part in pieces))
 
     for c in range(n_chip):
-        if passes(c).get(-1):
-            pl.when(chip == c)(functools.partial(pass_through, passes(c)[-1]))
-    q_rest = q_stage.at[1:n_seq]
-    pltpu.make_async_copy(q_rest, q_rest, q_recv).wait()
-
-    @pl.loop(0, 2 * chip + core + 1)
-    def _(i):
-        k = i - (1 + core)
-        here = k < 0
-        h, part = (k + 2) // 2, lax.rem(k + 2, 2)
-        if order(last) != [(m // 2 + 1, m % 2) for m in range(2 * last)]:
-            for m, (hop, which) in enumerate(order(last)):
-                h = jnp.where((chip == last) & (k == m), hop, h)
-                part = jnp.where((chip == last) & (k == m), which, part)
-        up, side = span - 2 * h, sibling - 2 * h
-        for c in range(n_chip):
-            for when, what in passes(c).items():
-                if when >= 0:
-                    pl.when((chip == c) & (k == when))(functools.partial(pass_through, what))
-
-        @pl.when(jnp.logical_not(here))
-        def _():
-            for g in range(half):
-                await_chunk(side, part * half + g)
-
-        @pl.when(here & (i == 1))
-        def _():
-            for g in range(n_g):
-                await_chunk(sibling, g)
-
-        only = jnp.where(i == 1, sibling, span)
-        absorb(
-            (jnp.where(here, only, up), jnp.where(here, 0, part)),
-            (jnp.where(here, only, side), jnp.where(here, 1, part)),
-        )
-
-    for g in list(range(1, n_g)) + [0]:
+        for k in range(2):
+            pl.when((chip == c) & (core == k))(functools.partial(run, c, k))
+
+    for g in reversed(range(n_g)):
         at = slice(g * rows, (g + 1) * rows)
         whole = jnp.sum(total[at, : min(HD, n_g * rows)], axis=-1, keepdims=True)
-        obuf[at, :] = (accum[at, :] / whole * gate_row[0:1, :]).astype(jnp.bfloat16)
+        obuf[at, :] = (accum[at, :] * (1.0 / whole) * gate_row[0:1, :]).astype(jnp.bfloat16)
         for s, _, _ in far_first:
             if s // per == g:
                 pltpu.make_async_remote_copy(
@@ -314,9 +364,10 @@
 
     drain(kv_stage.at[1:n_seq], kv_send)
     drain(q_stage.at[1:n_seq], q_send)
+    pl.when(chip < last)(functools.partial(drain, kv_stage.at[0:per], direct_send))
     for c in range(n_chip):
         passed = [h for h in range(c + 1) if not (wrap and h == last - 1)] if c < last else []
-        n_down = len(passed) * n_g + (n_g - n_wrap if wrap and c == 0 else 0)
+        n_down = len(passed) * n_g + (n_g - n_wrap if wrap and c == 0 else 0) - (n_direct if c < last else 0)
         if n_down:
             pl.when(chip == c)(functools.partial(drain, kv.at[0:n_down], down_send))
         pl.when((chip == c) & (core == 0))(functools.partial(drain, kv.at[0 : (c + 1) * n_g], side_send))
@@ -348,7 +399,7 @@
             pltpu.VMEM((tok, width), bf16),
             pltpu.VMEM((tok, width), bf16),
             pltpu.VMEM((tok, width), bf16),
-            pltpu.SMEM(timesteps.shape, timesteps.dtype),
+            pltpu.VMEM((1, 1), timesteps.dtype),
             pltpu.VMEM(history.shape, history.dtype),
             pltpu.VMEM(gate_weight.shape, bf16),
             pltpu.VMEM((n_seq, 2, tok, HD), bf16),
@@ -370,6 +421,7 @@
             pltpu.SemaphoreType.DMA,
             pltpu.SemaphoreType.DMA,
             pltpu.SemaphoreType.DMA,
+            pltpu.SemaphoreType.DMA,
             pltpu.SemaphoreType.DMA((n_g,)),
             pltpu.SemaphoreType.DMA,
             pltpu.SemaphoreType.DMA,
@@ -379,7 +431,7 @@
             collective_id=0, has_side_effects=True, vmem_limit_bytes=VLIM * 2**20
         ),
         name="attention",
-    )(queries, keys, values, timesteps, history, gate_weight)
+    )(queries, keys, values, timesteps.reshape(1, 1), history, gate_weight)
 
 
 def solution(mesh):

time: 45.2 us -> 43.9 us (0.971)
  Pallas kernels: 43.4 us -> 42.4 us
    pallas_call x1, Pallas kernels: 43.4 us -> 42.4 us  [body(): pl.pallas_call(functools.partial(kernel, n_span, n_x, n_z, n_g, wrap, tok...]
where the time goes in v4:
time: 43.9 us; the launch traced here: 43.7 us
  Pallas kernels  42.4 us (97%)
  local copies, waits for them, and re-layouts  0.66 us (2%)
  between operations  0.66 us (2%)
    pallas_call x1, Pallas kernels, body(): pl.pallas_call(functools.partial(kernel, n_span, n_x, n_z, n_g, wrap, tok...  42.4 us

profile of v4, /device:TPU:56, one launch (start us, length us, event | category | flops | bytes accessed | tf_op | source)
XLA Modules:
  0.0 43.7 jit_solution(17848565376072586255)
XLA Ops:
  0.7 42.4 %attention.1 = bf16[1,16,4096]{2,1,0:T(8,128)(2,1)S(1)} custom-call(bf16[1,16,4096]{2,1,0:T(8,128)(2,1)} %q_hbm.1, bf16[1,16,4096]{2,1,0:T(8,128)(2,1)} %k_hbm.1, bf16[1,16,4096]{2,1,0:T(8,128)(2,1)} %v_hbm.1, s32[1,1]{1,0:T(1,128)} %bitcast.1.steps_hbm, s32[1,256]{1,0:T(1,128)} %history_hbm.1, bf16[256,128]{1,0:T(8,128)(2,1)} %gatew_hbm.1), custom_call_target="tpu_custom_call" | custom-call | tf_op jit(solution)/shard_map/attention/pallas_call | solution.py:393
  43.1 0.7 %copy.8 = bf16[1,16,4096]{2,1,0:T(8,128)(2,1)} copy(bf16[1,16,4096]{2,1,0:T(8,128)(2,1)S(1)} %attention.1) | data formatting | bytes 262144

commit v5 on v4

--- a/solution.py
+++ b/solution.py
@@ -13,7 +13,7 @@
 RAISE = math.log2(math.e) / math.sqrt(HD)
 HIDDEN = -1e30
 VLIM = 60
-WG = 3
+WN = 2
 GN = 4
 
 
@@ -35,11 +35,12 @@
     q_hbm, k_hbm, v_hbm, steps_hbm, history_hbm, gatew_hbm,
     out_ref,
     q_in, k_in, v_in, steps, history, gatew, kv_stage, q_stage, kv, relay, qbuf, obuf, bias, gate_row, top, total, accum,
-    in_sem, kv_recv, kv_send, direct_send, q_recv, q_send, down_send, side_send, wrap_send, relay_recv, relay_send, o_recv, o_send,
+    in_sem, kv_recv, kv_send, direct_send, far_send, q_recv, q_send, down_send, side_send, wrap_send, relay_recv, relay_send, o_recv, o_send,
 ):
     n_seq = n_x * n_z
-    n_wrap = min(WG, n_g) if wrap else 0
     n_direct = 1
+    wrapped = range(n_direct, min(n_direct + WN, n_g)) if wrap else range(0)
+    straight = range(n_direct + len(wrapped), n_g) if wrap else range(0)
     per = n_seq // n_g
     rows = per * tok
     n_chip = n_span // 2
@@ -92,6 +93,8 @@
     if wrap:
         pl.when(chip == 0)(lambda: greet({"span": span + 2 * last}))
         pl.when(chip == last)(lambda: greet({"span": core}))
+        pl.when(chip == last)(lambda: greet_near({"span": core}))
+        others += (per - 1) * (chip == 0).astype(jnp.int32)
         pl.when(chip == 0)(lambda: greet(hop1))
         pl.when(chip == 1)(lambda: greet({"rep": 1 - video, "span": core}))
         pl.when(chip == 1)(lambda: greet(hop2))
@@ -106,17 +109,19 @@
     qbuf[0:tok, :] = q_stage[seq]
     pl.semaphore_wait(barrier, others)
 
-    def send_near():
+    def send_near(to, sent):
         for s, g, at in near:
             pltpu.make_async_remote_copy(
                 src_ref=kv_stage.at[ahead[s]],
                 dst_ref=kv.at[span * n_g + g, :, at, :],
-                send_sem=direct_send,
+                send_sem=sent,
                 recv_sem=kv_recv.at[span * n_g + g],
-                device_id={"span": span + 2, "seq": ahead[s]},
+                device_id={"span": to, "seq": ahead[s]},
             ).start()
 
-    pl.when(chip < last)(send_near)
+    pl.when(chip < last)(lambda: send_near(span + 2, direct_send))
+    if wrap:
+        pl.when(chip == 0)(lambda: send_near(span + 2 * last, far_send))
     for s, g, at in slots[1:]:
         pltpu.make_async_remote_copy(
             src_ref=kv_stage.at[ahead[s]],
@@ -241,7 +246,7 @@
             await_chunk(span, g, tok if g == 0 else 0)
         if g >= n_direct:
             pl.when(goes_on(0))(chunk_copy(span, g, down_send, {"span": span + 2}).start)
-        if g < n_wrap:
+        if g in wrapped:
             pl.when(chip == 0)(wrap_copy(g).start)
         pl.when(core == 0)(chunk_copy(span, g, side_send, {"span": sibling}).start)
 
@@ -257,12 +262,12 @@
             for g in halves(what[1]):
                 await_chunk(sibling - 2 * what[0], g)
         elif op == "relay":
-            if what[0] < n_wrap:
+            if what[0] in wrapped:
                 here = relay.at[what[0]]
                 pltpu.make_async_copy(here, here, relay_recv.at[what[0]]).wait()
                 relay_copy(what[0]).start()
-        elif op == "far":
-            for g in range(n_wrap, n_g) if wrap else []:
+        elif op == "straight":
+            for g in straight:
                 chunk_copy(span, g, down_send, {"span": span + 2 * last}).start()
         elif op == "queries":
             rest = q_stage.at[1:n_seq]
@@ -292,9 +297,9 @@
             return [("side", last - 1, part), ("side", last, part), ((d - 2 * (last - 1), part), (d - 2 * last, part))]
 
         start = [("queries",)] + whole(0)
-        relays = [[("relay", g)] for g in range(n_g)] + [[]] * 4
+        relays = [[("relay", g)] for g in wrapped] + [[]] * 4
         if c == 0:
-            return start[:1] + [("far",)] + start[1:] + (side(0) if k == 1 else [])
+            return start + (side(0) if k == 1 else []) + [("straight",)]
         if c == 1 and k == 0:
             return ([("take", 1, 0)] + start + relays[0] + [("take", 1, 1)] + relays[1] + side(1) + relays[2] + relays[3]
                     + up(1))
@@ -324,11 +329,11 @@
         @pl.loop(0, len(steps))
         def _(i):
             pieces = [[jnp.int32(0), jnp.int32(0)], [jnp.int32(0), jnp.int32(0)]]
-            for n, (waits, pair) in enumerate(steps):
+            for n, (before, pair) in enumerate(steps):
 
                 @pl.when(i == n)
                 def _():
-                    for one in waits:
+                    for one in before:
                         do(*one)
 
                 for piece, (distance, part) in zip(pieces, pair):
@@ -336,11 +341,14 @@
                     piece[1] = jnp.where(i == n, part, piece[1])
             absorb(*((span + distance, part) for distance, part in pieces))
 
+        for one in waits:
+            do(*one)
+
     for c in range(n_chip):
         for k in range(2):
             pl.when((chip == c) & (core == k))(functools.partial(run, c, k))
 
-    for g in reversed(range(n_g)):
+    for g in list(range(2, n_g)) + [1, 0]:
         at = slice(g * rows, (g + 1) * rows)
         whole = jnp.sum(total[at, : min(HD, n_g * rows)], axis=-1, keepdims=True)
         obuf[at, :] = (accum[at, :] * (1.0 / whole) * gate_row[0:1, :]).astype(jnp.bfloat16)
@@ -367,15 +375,18 @@
     pl.when(chip < last)(functools.partial(drain, kv_stage.at[0:per], direct_send))
     for c in range(n_chip):
         passed = [h for h in range(c + 1) if not (wrap and h == last - 1)] if c < last else []
-        n_down = len(passed) * n_g + (n_g - n_wrap if wrap and c == 0 else 0) - (n_direct if c < last else 0)
+        n_down = len(passed) * n_g - (n_direct if c < last else 0)
+        n_down += len(straight) if c == 0 else 0
         if n_down:
             pl.when(chip == c)(functools.partial(drain, kv.at[0:n_down], down_send))
         pl.when((chip == c) & (core == 0))(functools.partial(drain, kv.at[0 : (c + 1) * n_g], side_send))
         if c > 0:
             pl.when((chip == c) & (core == 1))(functools.partial(drain, kv.at[0 : c * n_g], side_send))
-    if n_wrap:
-        pl.when(chip == 0)(functools.partial(drain, relay.at[0:n_wrap], wrap_send))
-        pl.when(chip == 1)(functools.partial(drain, relay.at[0:n_wrap], relay_send))
+    if wrap:
+        if len(wrapped):
+            pl.when(chip == 0)(functools.partial(drain, relay.at[0 : len(wrapped)], wrap_send))
+            pl.when(chip == 1)(functools.partial(drain, relay.at[0 : len(wrapped)], relay_send))
+        pl.when(chip == 0)(functools.partial(drain, kv_stage.at[0:per], far_send))
     drain(obuf.at[tok:, :], o_send)
     drain(out_ref.at[0, :, 0 : (n_seq - 1) * HD], o_recv)
 
@@ -422,6 +433,7 @@
             pltpu.SemaphoreType.DMA,
             pltpu.SemaphoreType.DMA,
             pltpu.SemaphoreType.DMA,
+            pltpu.SemaphoreType.DMA,
             pltpu.SemaphoreType.DMA((n_g,)),
             pltpu.SemaphoreType.DMA,
             pltpu.SemaphoreType.DMA,

time: 43.9 us -> 43.6 us (level)
  Pallas kernels: 42.4 us -> 41.8 us
    pallas_call x1, Pallas kernels: 42.4 us -> 41.8 us  [body(): pl.pallas_call(functools.partial(kernel, n_span, n_x, n_z, n_g, wrap, tok...]
where the time goes in v5:
time: 43.6 us; the launch traced here: 43.1 us
  Pallas kernels  41.8 us (96%)
  local copies, waits for them, and re-layouts  0.66 us (2%)
  between operations  0.66 us (2%)
    pallas_call x1, Pallas kernels, body(): pl.pallas_call(functools.partial(kernel, n_span, n_x, n_z, n_g, wrap, tok...  41.8 us

profile of v5, /device:TPU:56, one launch (start us, length us, event | category | flops | bytes accessed | tf_op | source)
XLA Modules:
  0.0 43.1 jit_solution(7901225240499350884)
XLA Ops:
  0.7 41.8 %attention.1 = bf16[1,16,4096]{2,1,0:T(8,128)(2,1)S(1)} custom-call(bf16[1,16,4096]{2,1,0:T(8,128)(2,1)} %q_hbm.1, bf16[1,16,4096]{2,1,0:T(8,128)(2,1)} %k_hbm.1, bf16[1,16,4096]{2,1,0:T(8,128)(2,1)} %v_hbm.1, s32[1,1]{1,0:T(1,128)} %bitcast.1.steps_hbm, s32[1,256]{1,0:T(1,128)} %history_hbm.1, bf16[256,128]{1,0:T(8,128)(2,1)} %gatew_hbm.1), custom_call_target="tpu_custom_call" | custom-call | tf_op jit(solution)/shard_map/attention/pallas_call | solution.py:404
  42.5 0.7 %copy.8 = bf16[1,16,4096]{2,1,0:T(8,128)(2,1)} copy(bf16[1,16,4096]{2,1,0:T(8,128)(2,1)S(1)} %attention.1) | data formatting | bytes 262144

commit v6 on v5

--- a/solution.py
+++ b/solution.py
@@ -144,7 +144,7 @@
     n_freq = FREQ // 2
     k_index = lax.broadcasted_iota(jnp.int32, (8, n_freq), 1).astype(jnp.float32)
     freqs = jnp.exp(-math.log(10000.0) * k_index / n_freq)
-    angle = steps[...].astype(jnp.float32) * freqs
+    angle = steps[0].astype(jnp.float32) * freqs
     embedding = jnp.concatenate([jnp.cos(angle), jnp.sin(angle)], axis=-1).astype(jnp.bfloat16)
     gate_row[...] = jnp.dot(embedding, gatew[...], preferred_element_type=jnp.float32)
 
@@ -404,13 +404,13 @@
     return pl.pallas_call(
         functools.partial(kernel, n_span, n_x, n_z, n_g, wrap, tok),
         out_shape=pltpu.VMEM(queries.shape, bf16),
-        in_specs=[pl.BlockSpec(memory_space=pltpu.HBM)] * 6,
+        in_specs=[pl.BlockSpec(memory_space=pl.ANY)] * 6,
         out_specs=pl.BlockSpec(memory_space=pltpu.VMEM),
         scratch_shapes=[
             pltpu.VMEM((tok, width), bf16),
             pltpu.VMEM((tok, width), bf16),
             pltpu.VMEM((tok, width), bf16),
-            pltpu.VMEM((1, 1), timesteps.dtype),
+            pltpu.SMEM(timesteps.shape, timesteps.dtype),
             pltpu.VMEM(history.shape, history.dtype),
             pltpu.VMEM(gate_weight.shape, bf16),
             pltpu.VMEM((n_seq, 2, tok, HD), bf16),
@@ -443,7 +443,7 @@
             collective_id=0, has_side_effects=True, vmem_limit_bytes=VLIM * 2**20
         ),
         name="attention",
-    )(queries, keys, values, timesteps.reshape(1, 1), history, gate_weight)
+    )(queries, keys, values, timesteps, history, gate_weight)
 
 
 def solution(mesh):

time: 43.6 us -> 43.3 us (level)
  no operation moved by 1% of the time
where the time goes in v6:
time: 43.3 us; the launch traced here: 43.2 us
  Pallas kernels  41.9 us (97%)
  local copies, waits for them, and re-layouts  0.66 us (2%)
  between operations  0.66 us (2%)
    pallas_call x1, Pallas kernels, body(): pl.pallas_call(functools.partial(kernel, n_span, n_x, n_z, n_g, wrap, tok...  41.9 us

profile of v6, /device:TPU:56, one launch (start us, length us, event | category | flops | bytes accessed | tf_op | source)
XLA Modules:
  0.0 43.2 jit_solution(15693406967083310755)
XLA Ops:
  0.7 41.9 %attention.1 = bf16[1,16,4096]{2,1,0:T(8,128)(2,1)S(1)} custom-call(bf16[1,16,4096]{2,1,0:T(8,128)(2,1)} %q_hbm.1, bf16[1,16,4096]{2,1,0:T(8,128)(2,1)} %k_hbm.1, bf16[1,16,4096]{2,1,0:T(8,128)(2,1)} %v_hbm.1, s32[1]{0:T(128)S(6)} %copy.9.steps_hbm, s32[1,256]{1,0:T(1,128)} %history_hbm.1, bf16[256,128]{1,0:T(8,128)(2,1)} %gatew_hbm.1), custom_call_target="tpu_custom_call" | custom-call | tf_op jit(solution)/shard_map/attention/pallas_call | solution.py:404
  42.5 0.7 %copy.8 = bf16[1,16,4096]{2,1,0:T(8,128)(2,1)} copy(bf16[1,16,4096]{2,1,0:T(8,128)(2,1)S(1)} %attention.1) | data formatting | bytes 262144

commit v7 on v6

--- a/solution.py
+++ b/solution.py
@@ -312,7 +312,7 @@
         if k == 0:
             return ([("take", 1, 0)] + start + side(1) + [("take", 1, 1)] + up(1)
                     + [("take", 2, 0)] + side(2) + [("take", 3, 0)] + both_up(0)
-                    + [("take", 2, 1), ("take", 3, 1)] + side(3)
+                    + side(3) + [("take", 2, 1), ("take", 3, 1)]
                     + both_up(1))
         return (take_both(1) + start + up(1) + side(0) + take_both(2) + up(2) + side(1) + take_both(3) + up(3)
                 + both_side(0) + both_side(1))

time: 43.3 us -> 42.8 us (0.988)
  Pallas kernels: 41.9 us -> 41.1 us
    pallas_call x1, Pallas kernels: 41.9 us -> 41.1 us  [body(): pl.pallas_call(functools.partial(kernel, n_span, n_x, n_z, n_g, wrap, tok...]
where the time goes in v7:
time: 42.8 us; the launch traced here: 42.4 us
  Pallas kernels  41.1 us (96%)
  local copies, waits for them, and re-layouts  0.66 us (2%)
  between operations  0.66 us (2%)
    pallas_call x1, Pallas kernels, body(): pl.pallas_call(functools.partial(kernel, n_span, n_x, n_z, n_g, wrap, tok...  41.1 us

profile of v7, /device:TPU:56, one launch (start us, length us, event | category | flops | bytes accessed | tf_op | source)
XLA Modules:
  0.0 42.4 jit_solution(13463261449031964845)
XLA Ops:
  0.7 41.1 %attention.1 = bf16[1,16,4096]{2,1,0:T(8,128)(2,1)S(1)} custom-call(bf16[1,16,4096]{2,1,0:T(8,128)(2,1)} %q_hbm.1, bf16[1,16,4096]{2,1,0:T(8,128)(2,1)} %k_hbm.1, bf16[1,16,4096]{2,1,0:T(8,128)(2,1)} %v_hbm.1, s32[1]{0:T(128)S(6)} %copy.9.steps_hbm, s32[1,256]{1,0:T(1,128)} %history_hbm.1, bf16[256,128]{1,0:T(8,128)(2,1)} %gatew_hbm.1), custom_call_target="tpu_custom_call" | custom-call | tf_op jit(solution)/shard_map/attention/pallas_call | solution.py:404
  41.7 0.7 %copy.8 = bf16[1,16,4096]{2,1,0:T(8,128)(2,1)} copy(bf16[1,16,4096]{2,1,0:T(8,128)(2,1)S(1)} %attention.1) | data formatting | bytes 262144
